TPU v7x, 512 devices: a whole 4x4x16 slice. The times are simulated.
512 devices in a mesh: row: 32 (over x_lo, z), col: 16 (over x_hi, y, core).
Axes of the slice: x: 4 (x_hi: 2, x_lo: 2; x = x_hi * 2 + x_lo), y: 4, z: 16, core: 2. Of those that a mesh axis runs over, the one named last changes fastest.
Arguments:
- features: bfloat16 [65536, 128], P(('col', 'row')), may hold values from -6 to 6
- grad_out: bfloat16 [65536, 256], P(('row', 'col')), may hold values from -6 to 6
- row_scale: float32 [65536], P(('row', 'col')), may hold values from 0.00390625 to 0.0390625
- out_bias: float32 [256], replicated, may hold values from -3 to 3
- weight: bfloat16 [128, 256], replicated, may hold values from -0.5 to 0.5
- tile_vals: bfloat16 [32, 16, 128, 128, 128], P('row', 'col'), as said below
- tile_rows: int32 [32, 16, 128], P('row', 'col'), may hold values from 0 to 15, as said below
- tile_cols: int32 [32, 16, 128], P('row', 'col'), may hold values from 0 to 31, as said below
- tile_count: int32 [32, 16], P('row', 'col'), may hold values from 16 to 128, as said below
Outputs:
- output: bfloat16 [65536, 256], P(('row', 'col'))
- grad_features: bfloat16 [65536, 128], P(('col', 'row'))
- grad_weight: float32 [128, 256], replicated
Inputs may be any that keep to these rules, and one draw needn't show every extreme that they name: `tile_count`: every device holds from 128 // 8 (at least 1) to 128 tiles, and some device holds exactly 128; slots at and beyond a device's count hold no tile. The pairs (tile_rows, tile_cols) of one device's slots are all different. `tile_cols`: see tile_rows. `tile_vals`: about half of a tile's entries are zero.
All inputs are finite; a program needn't handle non-finite values.
Results may differ from a plain program's by a relative error of at most 0.029.
Values may be sent and summed in bfloat16 or wider, within the bound.
No kernel may reach another device: no remote copies, remote signals or barrier semaphores. Data moves between devices by JAX's collectives and lax.ppermute only.
A program may use at most 64 MiB of HBM per device.

v0:
```python
import jax
import jax.numpy as jnp
from jax import lax
from jax.sharding import PartitionSpec as P


def tile_sweep(
    values, slot_order, source_idx, target_idx, first, last, block_first, targets, source, transpose
):
    slot_count = values.shape[0]
    group_size = min(16, slot_count)
    rounds = (last - first + group_size - 1) // group_size
    edge = source.shape[1]
    width = source.shape[2]
    group_ids = jnp.arange(group_size, dtype=jnp.int32)

    def step(which, running):
        positions = first + which * group_size + group_ids
        clipped = jnp.take(slot_order, jnp.minimum(positions, slot_count - 1))
        tiles_now = jnp.take(values, clipped, axis=0)
        sources_now = jnp.take(source_idx, clipped)
        targets_now = jnp.take(target_idx, clipped)
        picked = jnp.take(source, sources_now, axis=0)
        if transpose:
            product = jnp.einsum(
                "tab,taw->tbw", tiles_now, picked, preferred_element_type=jnp.float32
            )
        else:
            product = jnp.einsum(
                "tab,tbw->taw", tiles_now, picked, preferred_element_type=jnp.float32
            )
        active = positions < last
        local_target = jnp.where(active, targets_now - block_first, 0)
        product = jnp.where(active[:, None, None], product, 0.0)
        return running.at[local_target].add(product)

    empty = jnp.zeros((targets, edge, width), jnp.float32)
    return lax.fori_loop(0, rounds, step, empty)


def on_device(
    features, grad_out, row_scale, out_bias, weight, tile_vals, tile_rows, tile_cols, tile_count
):
    row_devs = lax.axis_size("row")
    col_devs = lax.axis_size("col")
    own_nodes = features.shape[0]
    edge = tile_vals.shape[-1]
    slot_count = tile_vals.shape[2]
    row_blocks = own_nodes * col_devs // edge
    col_blocks = own_nodes * row_devs // edge
    width = weight.shape[1]
    values = tile_vals.reshape(slot_count, edge, edge)
    rows_idx = tile_rows.reshape(slot_count)
    cols_idx = tile_cols.reshape(slot_count)
    tile_total = tile_count.reshape(())
    slot_ids = jnp.arange(slot_count, dtype=jnp.int32)
    local_part = jnp.dot(features, weight, preferred_element_type=jnp.float32).astype(jnp.bfloat16)
    transformed = lax.all_gather(local_part, "row", axis=0, tiled=True)
    source_blocks = transformed.reshape(col_blocks, edge, width)
    partial_value = tile_sweep(
        values, slot_ids, cols_idx, rows_idx, 0, tile_total, 0, row_blocks, source_blocks, False
    )
    summed = lax.psum_scatter(
        partial_value.reshape(row_blocks * edge, width), "col", scatter_dimension=0, tiled=True
    )
    hidden = row_scale[:, None] * summed + out_bias[None, :]
    sigma = jax.nn.sigmoid(hidden)
    output = (hidden * sigma).astype(jnp.bfloat16)
    d_hidden = grad_out.astype(jnp.float32) * sigma * (1.0 + hidden * (1.0 - sigma))
    scaled = (row_scale[:, None] * d_hidden).astype(jnp.bfloat16)
    row_grads = lax.all_gather(scaled, "col", axis=0, tiled=True).reshape(row_blocks, edge, width)
    backward = tile_sweep(
        values, slot_ids, rows_idx, cols_idx, 0, tile_total, 0, col_blocks, row_grads, True
    )
    backward_term = backward.reshape(col_blocks * edge, width).astype(jnp.bfloat16)
    col_total = lax.psum_scatter(backward_term, "row", scatter_dimension=0, tiled=True).astype(
        jnp.float32
    )
    rounded = col_total.astype(jnp.bfloat16)
    grad_features = jnp.dot(rounded, weight.T, preferred_element_type=jnp.float32).astype(
        jnp.bfloat16
    )
    local_grad = jnp.einsum("nd,nf->df", features, rounded, preferred_element_type=jnp.float32)
    grad_weight = lax.psum(local_grad, ("row", "col"))
    return (output, grad_features, grad_weight)


def solution(mesh):
    return jax.shard_map(
        on_device,
        mesh=mesh,
        in_specs=(
            P(("col", "row"), None),
            P(("row", "col"), None),
            P(("row", "col")),
            P(),
            P(),
            P("row", "col", None, None, None),
            P("row", "col", None),
            P("row", "col", None),
            P("row", "col"),
        ),
        out_specs=(P(("row", "col"), None), P(("col", "row"), None), P()),
        check_vma=False,
    )
```

profile of v0, /device:TPU:1, one launch (start us, length us, event | category | flops | bytes accessed | tf_op | source)
XLA Modules:
  0.0 1116.2 jit_solution(14776645579166639647)
XLA Ops:
  7.2 0.8 copy-done
  8.0 1.5 convolution_convert_fusion
  10.3 118.7 %all-gather.3.cloned.1.call-done = bf16[4096,256]{1,0:T(8,128)(2,1)} async-done(((bf16[128,256]{1,0:T(8,128)(2,1)}), bf16[4096,256]{1,0:T(8,128)(2,1)}) %all-gather.3.cloned.1.call-update) | async-done | bytes 2097168 | tf_op jit(solution)/shard_map/all_gather | solution.py:58
  129.0 1.5 broadcast_in_dim.80
  130.5 26.3 %while.22 = (s32[]{:T(128)}, f32[16,128,256]{2,1,0:T(8,128)}, s32[]{:T(128)}, s32[]{:T(128)}, s32[128]{0:T(128)S(1)}, /*index=5*/bf16[128,128,128]{2,1,0:T(8,128...) while((s32[]{:T(128)}, f32[16,128,256]{2,1,0:T(8,128)}, s32[]{:T(128)}, ...), condition=%wide.region_2.5_spmd.clone, body=%wide.region_0.4_spmd.clone.sunk | while | flops 136056448 | bytes 21510396 | solution.py:38
  130.5 0.7 gather_fusion
  131.2 0.7 gather_fusion.2
  131.9 0.7 gather_fusion.1
  132.6 0.7 compare_select_fusion.17
  133.3 3.6 gather_fusion.4
  136.9 0.6 gather_fusion.3
  137.5 1.6 convolution_select_fusion.4
  139.0 4.4 scatter_fusion
  143.4 0.7 gather_fusion
  144.1 0.7 gather_fusion.2
  144.8 0.7 gather_fusion.1
  145.5 0.7 compare_select_fusion.17
  146.2 3.6 gather_fusion.4
  149.8 0.6 gather_fusion.3
  150.4 1.6 convolution_select_fusion.4
  151.9 4.9 scatter_fusion
  156.9 181.8 %reduce-scatter.3.cloned.1.call-done = f32[128,256]{1,0:T(8,128)} async-done(((f32[2048,256]{1,0:T(8,128)}), f32[128,256]{1,0:T(8,128)}) %reduce-scatter.3.cloned.1.call-update) | async-done | bytes 131088 | tf_op jit(solution)/shard_map/reduce_scatter | solution.py:63
  338.7 1.7 multiply_convert_fusion
  340.5 64.3 %all-gather.5.cloned.1.call-done = bf16[2048,256]{1,0:T(8,128)(2,1)} async-done(((bf16[128,256]{1,0:T(8,128)(2,1)}), bf16[2048,256]{1,0:T(8,128)(2,1)}) %all-gather.5.cloned.1.call-update) | async-done | bytes 1048592 | tf_op jit(solution)/shard_map/all_gather | solution.py:71
  404.8 2.5 broadcast_in_dim.81
  407.3 28.8 %while.23 = (s32[]{:T(128)}, f32[32,128,256]{2,1,0:T(8,128)}, s32[]{:T(128)}, s32[]{:T(128)}, s32[128]{0:T(128)S(1)}, /*index=5*/bf16[128,128,128]{2,1,0:T(8,128...) while((s32[]{:T(128)}, f32[32,128,256]{2,1,0:T(8,128)}, s32[]{:T(128)}, ...), condition=%wide.region_6.9_spmd.clone, body=%wide.region_4.8_spmd.clone.sunk | while | flops 136056448 | bytes 13121761 | solution.py:38
  407.3 0.7 gather_fusion.5
  408.0 0.7 gather_fusion.7
  408.7 0.7 gather_fusion.6
  409.3 0.7 compare_select_fusion.19
  410.0 3.6 gather_fusion.9
  413.7 1.8 gather_fusion.8
  415.5 1.6 convolution_select_fusion.5
  417.1 4.5 scatter_fusion.1
  421.6 0.7 gather_fusion.5
  422.3 0.7 gather_fusion.7
  423.0 0.7 gather_fusion.6
  423.6 0.7 compare_select_fusion.19
  424.3 3.6 gather_fusion.9
  428.0 1.8 gather_fusion.8
  429.8 1.6 convolution_select_fusion.5
  431.4 4.6 scatter_fusion.1
  436.1 3.8 convert_element_type.27
  440.0 200.2 %reduce-scatter.5.cloned.1.call-done = bf16[128,256]{1,0:T(8,128)(2,1)} async-done(((bf16[4096,256]{1,0:T(8,128)(2,1)}), bf16[128,256]{1,0:T(8,128)(2,1)}) %reduce-scatter.5.cloned.1.call-update) | async-done | bytes 65552 | tf_op jit(solution)/shard_map/reduce_scatter | solution.py:76
  640.2 1.7 convolution_bitcast_fusion
  641.9 1.6 convolution_convert_fusion.1
  643.5 464.4 %all-reduce.2.cloned.1.call-done = f32[128,256]{0,1:T(8,128)} async-done(((f32[128,256]{0,1:T(8,128)}), f32[128,256]{0,1:T(8,128)}) %all-reduce.2.cloned.1.call-update) | async-done | bytes 131088 | tf_op jit(solution)/shard_map/psum | solution.py:84
  1108.0 1.7 copy.15
  (55 shorter events, 0.5 us)
Async XLA Ops:
  7.2 0.8 copy-start
  7.2 123.3 %copy-start.2 = (s32[1,1,128]{2,1,0:T(1,128)S(1)}, s32[1,1,128]{2,1,0:T(1,128)}, u32[]{:S(2)}) copy-start(s32[1,1,128]{2,1,0:T(1,128)} %param.24) | copy-start | bytes 1540
  7.2 123.3 %copy-start.1 = (s32[1,1,128]{2,1,0:T(1,128)S(1)}, s32[1,1,128]{2,1,0:T(1,128)}, u32[]{:S(2)}) copy-start(s32[1,1,128]{2,1,0:T(1,128)} %param.23) | copy-start | bytes 1540
  7.2 121.8 %all-gather.3.cloned.1.call-start = ((), (), s32[]{:S(2)}) async-start(), calls=%async_computation.2 | async-start | bytes 2162688 | tf_op jit(solution)/shard_map/all_gather | solution.py:58
  9.6 329.1 %reduce-scatter.3.cloned.1.call-start = ((), (), s32[]{:S(2)}) async-start(), calls=%async_computation.3 | async-start | bytes 2228224 | tf_op jit(solution)/shard_map/reduce_scatter | solution.py:63
  131.2 5.7 copy-start.3
  144.1 5.7 copy-start.3
  156.8 181.9 %copy-start.5 = (bf16[128,256]{1,0:T(8,128)(2,1)S(1)}, bf16[128,256]{1,0:T(8,128)(2,1)}, u32[]{:S(2)}) copy-start(bf16[128,256]{1,0:T(8,128)(2,1)} %param.18) | copy-start | bytes 196612
  156.8 181.9 %copy-start.6 = (f32[256]{0:T(256)S(1)}, f32[256]{0:T(256)}, u32[]{:S(2)}) copy-start(f32[256]{0:T(256)} %param.20) | copy-start | bytes 3076
  156.8 181.9 %copy-start.7 = (f32[128]{0:T(128)S(1)}, f32[128]{0:T(128)}, u32[]{:S(2)}) copy-start(f32[128]{0:T(128)} %param.19) | copy-start | bytes 1540
  156.9 248.0 %all-gather.5.cloned.1.call-start = ((), (), s32[]{:S(2)}) async-start(), calls=%async_computation.4 | async-start | bytes 1114112 | tf_op jit(solution)/shard_map/all_gather | solution.py:71
  340.4 299.7 %reduce-scatter.5.cloned.1.call-start = ((), (), s32[]{:S(2)}) async-start(), calls=%async_computation.5 | async-start | bytes 2162688 | tf_op jit(solution)/shard_map/reduce_scatter | solution.py:76
  439.9 200.3 %copy-start.4 = (bf16[128,128]{1,0:T(8,128)(2,1)S(1)}, bf16[128,128]{1,0:T(8,128)(2,1)}, u32[]{:S(2)}) copy-start(bf16[128,128]{1,0:T(8,128)(2,1)} %param.17) | copy-start | bytes 98308
  439.9 668.0 %all-reduce.2.cloned.1.call-start = ((), (), s32[]{:S(2)}) async-start(), calls=%async_computation.6 | async-start | bytes 262144 | tf_op jit(solution)/shard_map/psum | solution.py:84
Sparse Core Ops, SparseCore 0:
  10.7 118.2 all-gather.2
  157.0 181.6 reduce-scatter.2
  343.2 61.6 all-gather.4
  440.0 200.1 reduce-scatter.4
  646.1 461.8 all-reduce.1
where the time goes:
time: 1120 us
  waiting for transfers between devices  1030 us (92%)
  local copies, waits for them, and re-layouts  33.7 us (3%)
  other arithmetic  26.7 us (2%)
  between operations  14.5 us (1%)
    psum x1, waiting for transfers between devices, on_device(): grad_weight = lax.psum(local_grad, ('row', 'col'))  464 us
    reduce_scatter x1, waiting for transfers between devices, on_device(): lax.psum_scatter(backward_term, 'row', scatter_dimension=0, tiled=True)  200 us
    reduce_scatter x1, waiting for transfers between devices, on_device(): lax.psum_scatter(partial_value.reshape(row_blocks * edge, width), 'col',...  182 us
    all_gather x1, waiting for transfers between devices, on_device(): transformed = lax.all_gather(local_part, 'row', axis=0, tiled=True)  119 us
    all_gather x1, waiting for transfers between devices, on_device(): lax.all_gather(scaled, 'col', axis=0, tiled=True)  64.3 us
  transfers between devices with their start and end apart: 5, of which 5 were waited for; matrix products, arithmetic and copies ran while one was open for 0% of the time, Pallas kernels for 0%

commit v1 on v0

v1 whole, which is shorter than its diff:
```python
import jax
import jax.numpy as jnp
from jax import lax
from jax.experimental import pallas as pl
from jax.experimental.pallas import tpu as pltpu
from jax.sharding import Mesh
from jax.sharding import PartitionSpec as P

F32 = jnp.float32
BF16 = jnp.bfloat16
Z = ("zh", "zl")
ROW = ("xl",) + Z
COL = ("xh", "y", "core")
AXES = ROW + COL
SIZES = (2, 4, 4, 2, 4, 2)

E = 128
WIDE = 256
SLOTS = 128
GROUP = 16
CHUNKS = SLOTS // GROUP
NZ, NX, NC = 16, 2, 16
NR = NX * NZ
GW = 32
PACK = E + GW

ANY = pl.BlockSpec(memory_space=pl.ANY)
VMEM = pl.BlockSpec(memory_space=pltpu.VMEM)
SMEM = pl.BlockSpec(memory_space=pltpu.SMEM)
PARAMS = pltpu.CompilerParams(vmem_limit_bytes=40 * 1024 * 1024)


def split(x):
    high = x.astype(BF16)
    return high, (x - high.astype(F32)).astype(BF16)


def pack_weight_grad(piece):
    flat = jnp.concatenate([piece[:, :E], piece[:, E:]], axis=0)
    high, low = split(flat)
    return jnp.concatenate([high, low], axis=0)


def unpack_weight_grad(packed):
    wide = packed.astype(F32)
    return wide[:16] + wide[16:]


def sweep(count, chunk_copies, tile_product, add):
    def chunk_step(c, carry):
        chunk_copies(c).wait()
        left = count - c * GROUP

        @pl.when(left >= GROUP)
        def _():
            for u0 in range(0, GROUP, 4):
                products = [tile_product(c, u, c * GROUP + u) for u in range(u0, u0 + 4)]
                for k, product in enumerate(products):
                    add(c * GROUP + u0 + k, product)

        @pl.when(left < GROUP)
        def _():
            def one(u, inner):
                add(c * GROUP + u, tile_product(c, u, c * GROUP + u))
                return inner

            lax.fori_loop(0, left, one, 0)

        return carry

    lax.fori_loop(0, CHUNKS, chunk_step, 0)


def forward_kernel(count, rows, cols, own, tiles, mine, peer, out, held, source, total, tile_sem, source_sem):
    def tile_copy(c):
        return pltpu.make_async_copy(tiles.at[c], held.at[c], tile_sem.at[c])

    near = pltpu.make_async_copy(mine, source.at[pl.ds(0, NZ)], source_sem.at[0])
    far = pltpu.make_async_copy(peer, source.at[pl.ds(NZ, NZ)], source_sem.at[1])
    near.start()
    far.start()
    for c in range(CHUNKS):
        tile_copy(c).start()
    total[...] = jnp.zeros_like(total)
    flip = own[0] * NZ
    near.wait()
    far.wait()

    def product(c, u, t):
        place = jnp.bitwise_xor(cols[t], flip)
        return jnp.dot(held[c, u], source[place], preferred_element_type=F32)

    def add(t, value):
        total[rows[t]] += value

    sweep(count[0], tile_copy, product, add)
    out[...] = total[...].astype(BF16)


def node_kernel(terms, scale, bias, weight, grad_out, output, pack):
    gathered = terms[0].astype(F32)
    for k in range(1, NC):
        gathered = gathered + terms[k].astype(F32)
    high, low = split(gathered)
    w = weight[...]
    summed = jnp.dot(high, w, preferred_element_type=F32) + jnp.dot(low, w, preferred_element_type=F32)
    r = scale[...]
    hidden = r * summed + bias[...]
    s = jax.nn.sigmoid(hidden)
    output[...] = (hidden * s).astype(BF16)
    d_hidden = grad_out[...].astype(F32) * s * (1.0 + hidden * (1.0 - s))
    scaled = (r * d_hidden).astype(BF16)
    back = lax.dot_general(w, scaled, (((1,), (1,)), ((), ())), preferred_element_type=F32).astype(BF16)
    first = (((0,), (0,)), ((), ()))
    grad = lax.dot_general(high, scaled, first, preferred_element_type=F32)
    grad = grad + lax.dot_general(low, scaled, first, preferred_element_type=F32)
    for k in range(NC):
        pack[k, pl.ds(0, E)] = back
        pack[k, pl.ds(E, GW)] = pack_weight_grad(grad[8 * k : 8 * k + 8])


def backward_kernel(count, rows, cols, own, tiles, packed, keep, send, held, source, total, tile_sem, source_sem):
    def tile_copy(c):
        return pltpu.make_async_copy(tiles.at[c], held.at[c], tile_sem.at[c])

    arrive = pltpu.make_async_copy(packed, source, source_sem.at[0])
    arrive.start()
    for c in range(CHUNKS):
        tile_copy(c).start()
    total[...] = jnp.zeros_like(total)
    flip = own[0] * NZ
    arrive.wait()

    def product(c, u, t):
        return jnp.dot(source[rows[t], pl.ds(0, E)], held[c, u], preferred_element_type=F32)

    def add(t, value):
        total[jnp.bitwise_xor(cols[t], flip)] += value

    sweep(count[0], tile_copy, product, add)
    grad = unpack_weight_grad(source[0, pl.ds(E, GW)])
    for k in range(1, NC):
        grad = grad + unpack_weight_grad(source[k, pl.ds(E, GW)])
    high, low = split(grad)
    for z in range(NZ):
        keep[pl.ds(z * E, E)] = total[z].astype(BF16)
        send[pl.ds(z * E, E)] = total[NZ + z].astype(BF16)
    for ref in (keep, send):
        ref[pl.ds(NZ * E, 16)] = high
        ref[pl.ds(NZ * E + 16, 16)] = low


def pair_kernel(keep, came, pack):
    for z in range(NZ):
        rows = pl.ds(z * E, E)
        pack[z, pl.ds(0, E)] = (keep[rows].astype(F32) + came[rows].astype(F32)).astype(BF16)
    tail = pl.ds(NZ * E, GW)
    high, low = split(unpack_weight_grad(keep[tail]) + unpack_weight_grad(came[tail]))
    for z in range(NZ):
        pack[z, pl.ds(E, 16)] = high
        pack[z, pl.ds(E + 16, 16)] = low


def last_kernel(terms, grad_features, grad_piece):
    value = terms[0].astype(F32)
    for z in range(1, NZ):
        value = value + terms[z].astype(F32)
    grad_features[...] = value[:E].T.astype(BF16)
    both = value[E : E + 16] + value[E + 16 : E + 32]
    piece = jnp.concatenate([both[:8], both[8:]], axis=1)
    for k in range(NC):
        grad_piece[k] = piece


def shape(dims, kind=BF16):
    return jax.ShapeDtypeStruct(dims, kind)


def on_device(features, grad_out, row_scale, out_bias, weight, tile_vals, tile_rows, tile_cols, tile_count):
    tiles = tile_vals.reshape(CHUNKS, GROUP, E, E)
    rows = tile_rows.reshape(SLOTS)
    cols = tile_cols.reshape(SLOTS)
    count = tile_count.reshape(1)
    own = lax.axis_index("xl").astype(jnp.int32).reshape(1)
    swap = [(0, 1), (1, 0)]

    copies = jnp.broadcast_to(features[None], (NZ, E, E))
    mine = lax.all_to_all(copies, Z, 0, 0, tiled=True)
    peer = lax.ppermute(mine, "xl", swap)
    sems = [pltpu.SemaphoreType.DMA((CHUNKS,)), pltpu.SemaphoreType.DMA((2,))]
    partial = pl.pallas_call(
        forward_kernel,
        out_shape=shape((NC, E, E)),
        in_specs=[SMEM] * 4 + [ANY] * 3,
        out_specs=VMEM,
        scratch_shapes=[
            pltpu.VMEM((CHUNKS, GROUP, E, E), BF16),
            pltpu.VMEM((NR, E, E), BF16),
            pltpu.VMEM((NC, E, E), F32),
        ]
        + sems,
        compiler_params=PARAMS,
        name="forward_sweep",
    )(count, rows, cols, own, tiles, mine, peer)
    terms = lax.all_to_all(partial, COL, 0, 0, tiled=True)
    output, pack = pl.pallas_call(
        node_kernel,
        out_shape=(shape((E, WIDE)), shape((NC, PACK, E))),
        in_specs=[VMEM] * 5,
        out_specs=(VMEM, VMEM),
        compiler_params=PARAMS,
        name="node_update",
    )(terms, row_scale.reshape(E, 1), out_bias.reshape(1, WIDE), weight, grad_out)
    packed = lax.all_to_all(pack, COL, 0, 0, tiled=True)
    line = shape((NZ * E + GW, E))
    keep, send = pl.pallas_call(
        backward_kernel,
        out_shape=(line, line),
        in_specs=[SMEM] * 4 + [ANY] * 2,
        out_specs=(VMEM, VMEM),
        scratch_shapes=[
            pltpu.VMEM((CHUNKS, GROUP, E, E), BF16),
            pltpu.VMEM((NC, PACK, E), BF16),
            pltpu.VMEM((NR, E, E), F32),
        ]
        + sems,
        compiler_params=PARAMS,
        name="backward_sweep",
    )(count, rows, cols, own, tiles, packed)
    came = lax.ppermute(send, "xl", swap)
    pairs = pl.pallas_call(
        pair_kernel,
        out_shape=shape((NZ, PACK, E)),
        in_specs=[VMEM] * 2,
        out_specs=VMEM,
        compiler_params=PARAMS,
        name="pair_sum",
    )(keep, came)
    last = lax.all_to_all(pairs, Z, 0, 0, tiled=True)
    grad_features, piece = pl.pallas_call(
        last_kernel,
        out_shape=(shape((E, E)), shape((NC, 8, WIDE), F32)),
        in_specs=[VMEM],
        out_specs=(VMEM, VMEM),
        compiler_params=PARAMS,
        name="last_sum",
    )(last)
    grad_weight = lax.all_to_all(piece, COL, 0, 0, tiled=True).reshape(E, WIDE)
    return output, grad_features, grad_weight


def solution(mesh):
    fine = Mesh(mesh.devices.reshape(SIZES), AXES)
    by_row = ROW + COL
    by_col = COL + ROW
    return jax.shard_map(
        on_device,
        mesh=fine,
        in_specs=(
            P(by_col, None),
            P(by_row, None),
            P(by_row),
            P(),
            P(),
            P(ROW, COL, None, None, None),
            P(ROW, COL, None),
            P(ROW, COL, None),
            P(ROW, COL),
        ),
        out_specs=(P(by_row, None), P(by_col, None), P()),
        check_vma=False,
    )
```

time: 1120 us -> 184 us (0.16)
  waiting for transfers between devices: 1030 us -> 28.6 us
  blocking collectives: 0 us -> 115 us
  other arithmetic: 26.7 us -> 0 us
  local copies, waits for them, and re-layouts: 33.7 us -> 7.38 us
  starting transfers between devices: 0.2 us -> 24 us
  between operations: 14.5 us -> 1.38 us
    psum x1 -> x0, waiting for transfers between devices: 464 us -> none  [on_device(): grad_weight = lax.psum(local_grad, ('row', 'col'))]
    reduce_scatter x2 -> x0, waiting for transfers between devices: 382 us -> none  [the longest x1 200 us: on_device(): lax.psum_scatter(backward_term, 'row', scatter_dimension=0, tiled=True)]
    all_gather x2 -> x0, waiting for transfers between devices: 183 us -> none  [the longest x1 119 us: on_device(): transformed = lax.all_gather(local_part, 'row', axis=0, tiled=True)]
    all_to_all x0 -> x4, blocking collectives: none -> 115 us  [the longest x1 43.9 us: on_device(): last = lax.all_to_all(pairs, Z, 0, 0, tiled=True)]
    gather x20 -> x0, local copies, waits for them, and re-layouts: 27.3 us -> none  [the longest x4 14.5 us: step(): tiles_now = jnp.take(values, clipped, axis=0)]
    scatter-add x4 -> x0, other arithmetic: 18.4 us -> none  [step(): return running.at[local_target].add(product)]
    ppermute x0 -> x2, waiting for transfers between devices: none -> 17.4 us  [the longest x1 11.3 us: on_device(): came = lax.ppermute(send, 'xl', swap)]
    all_to_all x0 -> x1, starting transfers between devices: none -> 16.9 us  [on_device(): terms = lax.all_to_all(partial, COL, 0, 0, tiled=True)]
  transfers between devices with their start and end apart: 5 -> 3, of which waited for: 5 -> 3; matrix products, arithmetic and copies ran while one was open for 0% -> 0% of each run, Pallas kernels for 0% -> 0%
where the time goes in v1:
time: 184 us
  blocking collectives  115 us (62%)
  waiting for transfers between devices  28.6 us (16%)
  starting transfers between devices  24 us (13%)
  local copies, waits for them, and re-layouts  7.38 us (4%)
  Pallas kernels  6.79 us (4%)
    all_to_all x1, blocking collectives, on_device(): last = lax.all_to_all(pairs, Z, 0, 0, tiled=True)  43.9 us
    all_to_all x1, blocking collectives, on_device(): mine = lax.all_to_all(copies, Z, 0, 0, tiled=True)  38.4 us
    all_to_all x1, blocking collectives, on_device(): packed = lax.all_to_all(pack, COL, 0, 0, tiled=True)  16.9 us
    all_to_all x1, starting transfers between devices, on_device(): terms = lax.all_to_all(partial, COL, 0, 0, tiled=True)  16.9 us
    all_to_all x1, blocking collectives, on_device(): grad_weight = lax.all_to_all(piece, COL, 0, 0, tiled=True).reshape(E, WIDE)  16.2 us
    ppermute x1, waiting for transfers between devices, on_device(): came = lax.ppermute(send, 'xl', swap)  11.3 us
    all_to_all x1, waiting for transfers between devices, on_device(): terms = lax.all_to_all(partial, COL, 0, 0, tiled=True)  11.2 us
    unnamed x21, local copies, waits for them, and re-layouts  6.37 us
  transfers between devices with their start and end apart: 3, of which 3 were waited for; matrix products, arithmetic and copies ran while one was open for 0% of the time, Pallas kernels for 0%

profile of v1, /device:TPU:1, one launch (start us, length us, event | category | flops | bytes accessed | tf_op | source)
XLA Modules:
  0.0 183.5 jit_solution(6102458656498442462)
XLA Ops:
  0.6 0.0 copy-start.9
  0.6 0.0 copy-start.2
  0.7 0.0 copy-start.8
  0.7 0.0 copy-start.3
  0.7 0.9 broadcast_in_dim.2
  1.6 38.4 %all_to_all.25.mine = bf16[16,128,128]{2,1,0:T(8,128)(2,1)S(1)} all-to-all(bf16[16,128,128]{2,1,0:T(8,128)(2,1)S(1)} %broadcast_in_dim.2), channel_id=1, replica_groups=mesh['xl'=2,'zh'=4,'zl'=4,'xh'=2,'y'=4,'core'=2] {'zh','zl'}, dimensions={0} | all-to-all | bytes 1048576 | tf_op jit(solution)/shard_map/all_to_all | solution.py:188
  39.9 3.1 %collective-permute-start = (bf16[16,128,128]{2,1,0:T(8,128)(2,1)S(1)}, bf16[16,128,128]{2,1,0:T(8,128)(2,1)S(1)}, u32[]{:S(2)}, u32[]{:S(2)}) collective-permute-start(bf16[16,128,128]{2,1,0:T(8,128)(2,1)S(1)} %all_to_all.25.mine), channel_id=1, source_target_pairs={{0,256},{256,0},{1,257},{257,1},{2,258},{258,2},{3,259},{259,3},{4... | collective-permute-start | bytes 1572872 | tf_op jit(solution)/shard_map/ppermute | solution.py:189
  43.7 6.1 %collective-permute-done.peer = bf16[16,128,128]{2,1,0:T(8,128)(2,1)S(1)} collective-permute-done((bf16[16,128,128]{2,1,0:T(8,128)(2,1)S(1)}, bf16[16,128,128]{2,1,0:T(8,128)(2,1)S(1)}, u32[]{:S(2)}, u32[]{:S(2)}) %collective-permute-start) | collective-permute-done | bytes 524320 | tf_op jit(solution)/shard_map/ppermute | solution.py:189
  49.9 0.0 copy-start
  49.9 2.2 %copy-done = bf16[1,1,128,128,128]{4,3,2,1,0:T(8,128)(2,1)S(1)} copy-done((bf16[1,1,128,128,128]{4,3,2,1,0:T(8,128)(2,1)S(1)}, bf16[1,1,128,128,128]{4,3,2,1,0:T(8,128)(2,1)}, u32[]{:S(2)}) %copy-start) | copy-done | bytes 4194328
  52.1 0.0 copy-start.4
  52.1 0.7 copy-done.4
  52.7 0.0 copy-start.6
  52.7 0.7 copy-done.6
  53.4 0.0 copy-start.5
  53.4 0.0 copy-start.7
  53.4 2.7 %forward_sweep.1 = bf16[16,128,128]{2,1,0:T(8,128)(2,1)} custom-call(s32[1]{0:T(128)} %bitcast.8.count, s32[128]{0:T(128)S(1)} %bitcast.12, s32[128]{0:T(128)S(1)} %bitcast.14, s32[1]{0:T(128)} %bitcast.3.own, bf16[8,16,128,128]{3,2,1,0:T(8,128)(2,1)S(1)} %bitcast.10, bf16[16,128,128]{2,1,0:T(8,128)(2,1)S(1)} %all_to_all.25.mine, ...), custom_call_target="tpu_custom_call" | custom-call | tf_op jit(solution)/shard_map/forward_sweep/pallas_call | solution.py:191
  56.1 16.9 %all-to-all-start.1 = ((bf16[16,128,128]{2,1,0:T(8,128)(2,1)}), bf16[16,128,128]{2,1,0:T(8,128)(2,1)S(1)}, u32[]{:S(2)}, u32[]{:S(2)}) async-start(bf16[16,128,128]{2,1,0:T(8,128)(2,1)} %forward_sweep.1), calls=%async_computation.1 | async-start | bytes 1048576 | tf_op jit(solution)/shard_map/all_to_all | solution.py:205
  73.0 0.0 copy-done.9
  73.0 0.1 copy.12.scale
  73.1 11.2 %all-to-all-done.1.terms = bf16[16,128,128]{2,1,0:T(8,128)(2,1)S(1)} async-done(((bf16[16,128,128]{2,1,0:T(8,128)(2,1)}), bf16[16,128,128]{2,1,0:T(8,128)(2,1)S(1)}, u32[]{:S(2)}, u32[]{:S(2)}) %all-to-all-start.1) | async-done | bytes 524320 | tf_op jit(solution)/shard_map/all_to_all | solution.py:205
  84.3 0.0 copy-done.2
  84.3 0.0 copy-done.8
  84.3 0.0 copy-done.3
  84.3 0.9 node_update.1
  85.2 16.9 %all_to_all.26.packed = bf16[16,160,128]{2,1,0:T(8,128)(2,1)S(1)} all-to-all(bf16[16,160,128]{2,1,0:T(8,128)(2,1)S(1)} %get-tuple-element.10), channel_id=1, replica_groups=mesh['xl'=2,'zh'=4,'zl'=4,'xh'=2,'y'=4,'core'=2] {'xh','y','core'}, dimensions={0} | all-to-all | bytes 1310720 | tf_op jit(solution)/shard_map/all_to_all | solution.py:214
  102.1 0.0 copy-done.5
  102.1 0.0 copy-done.7
  102.1 0.0 copy-start.1
  102.1 2.2 %copy-done.1 = bf16[1,1,128,128,128]{4,3,2,1,0:T(8,128)(2,1)S(1)} copy-done((bf16[1,1,128,128,128]{4,3,2,1,0:T(8,128)(2,1)S(1)}, bf16[1,1,128,128,128]{4,3,2,1,0:T(8,128)(2,1)}, u32[]{:S(2)}) %copy-start.1) | copy-done | bytes 4194328
  104.3 2.2 %backward_sweep.1 = (bf16[2080,128]{1,0:T(8,128)(2,1)S(1)}, bf16[2080,128]{1,0:T(8,128)(2,1)S(1)}) custom-call(s32[1]{0:T(128)} %bitcast.9.count, s32[128]{0:T(128)S(1)} %bitcast.13, s32[128]{0:T(128)S(1)} %bitcast.15, s32[1]{0:T(128)} %bitcast.3.own, bf16[8,16,128,128]{3,2,1,0:T(8,128)(2,1)S(1)} %bitcast.11, bf16[16,160,128]{2,1,0:T(8,128)(2,1)S(1)} %all_to_all.26.packed), custom_call_target="tpu_custom_call" | custom-call | tf_op jit(solution)/shard_map/backward_sweep/pallas_call | solution.py:216
  106.5 4.1 %collective-permute-start.1 = (bf16[2080,128]{1,0:T(8,128)(2,1)S(1)}, bf16[2080,128]{1,0:T(8,128)(2,1)S(1)}, u32[]{:S(2)}, u32[]{:S(2)}) collective-permute-start(bf16[2080,128]{1,0:T(8,128)(2,1)S(1)} %get-tuple-element.12), channel_id=1, source_target_pairs={{0,256},{256,0},{1,257},{257,1},{2,258},{258,2},{3,259},{259,3},{4... | collective-permute-start | bytes 1597448 | tf_op jit(solution)/shard_map/ppermute | solution.py:230
  110.6 11.3 %collective-permute-done.1.came = bf16[2080,128]{1,0:T(8,128)(2,1)S(1)} collective-permute-done((bf16[2080,128]{1,0:T(8,128)(2,1)S(1)}, bf16[2080,128]{1,0:T(8,128)(2,1)S(1)}, u32[]{:S(2)}, u32[]{:S(2)}) %collective-permute-start.1) | collective-permute-done | bytes 532512 | tf_op jit(solution)/shard_map/ppermute | solution.py:230
  121.9 0.1 pair_sum.1
  122.0 43.9 %all_to_all.27.terms = bf16[16,160,128]{2,1,0:T(8,128)(2,1)S(1)} all-to-all(bf16[16,160,128]{2,1,0:T(8,128)(2,1)S(1)} %pair_sum.1), channel_id=1, replica_groups=mesh['xl'=2,'zh'=4,'zl'=4,'xh'=2,'y'=4,'core'=2] {'zh','zl'}, dimensions={0} | all-to-all | bytes 1310720 | tf_op jit(solution)/shard_map/all_to_all | solution.py:239
  165.9 0.8 last_sum.1
  166.7 16.2 %all_to_all.28 = f32[16,8,256]{2,1,0:T(8,128)S(1)} all-to-all(f32[16,8,256]{2,1,0:T(8,128)S(1)} %get-tuple-element.14), channel_id=1, replica_groups=mesh['xl'=2,'zh'=4,'zl'=4,'xh'=2,'y'=4,'core'=2] {'xh','y','core'}, dimensions={0} | all-to-all | bytes 262144 | tf_op jit(solution)/shard_map/all_to_all | solution.py:248
  182.9 0.7 copy.15
Async XLA Ops:
  0.6 72.4 %copy-start.9 = (f32[128]{0:T(128)S(1)}, f32[128]{0:T(128)}, u32[]{:S(2)}) copy-start(f32[128]{0:T(128)} %param.11) | copy-start | bytes 1540
  0.6 83.6 %copy-start.2 = (bf16[128,256]{1,0:T(8,128)(2,1)S(1)}, bf16[128,256]{1,0:T(8,128)(2,1)}, u32[]{:S(2)}) copy-start(bf16[128,256]{1,0:T(8,128)(2,1)} %weight.1) | copy-start | bytes 196612
  0.7 83.6 %copy-start.8 = (f32[256]{0:T(256)S(1)}, f32[256]{0:T(256)}, u32[]{:S(2)}) copy-start(f32[256]{0:T(256)} %param.12) | copy-start | bytes 3076
  0.7 83.6 %copy-start.3 = (bf16[128,256]{1,0:T(8,128)(2,1)S(1)}, bf16[128,256]{1,0:T(8,128)(2,1)}, u32[]{:S(2)}) copy-start(bf16[128,256]{1,0:T(8,128)(2,1)} %grad_out.1) | copy-start | bytes 196612
  39.9 9.9 %collective-permute-start = (bf16[16,128,128]{2,1,0:T(8,128)(2,1)S(1)}, bf16[16,128,128]{2,1,0:T(8,128)(2,1)S(1)}, u32[]{:S(2)}, u32[]{:S(2)}) collective-permute-start(bf16[16,128,128]{2,1,0:T(8,128)(2,1)S(1)} %all_to_all.25.mine), channel_id=1, source_target_pairs={{0,256},{256,0},{1,257},{257,1},{2,258},{258,2},{3,259},{259,3},{4... | collective-permute-start | bytes 1572872 | tf_op jit(solution)/shard_map/ppermute | solution.py:189
  49.9 2.2 %copy-start = (bf16[1,1,128,128,128]{4,3,2,1,0:T(8,128)(2,1)S(1)}, bf16[1,1,128,128,128]{4,3,2,1,0:T(8,128)(2,1)}, u32[]{:S(2)}) copy-start(bf16[1,1,128,128,128]{4,3,2,1,0:T(8,128)(2,1)} %param.14) | copy-start | bytes 12582916
  52.1 0.7 copy-start.4
  52.7 0.7 copy-start.6
  53.4 48.7 %copy-start.5 = (s32[1,1,128]{2,1,0:T(1,128)S(1)}, s32[1,1,128]{2,1,0:T(1,128)}, u32[]{:S(2)}) copy-start(s32[1,1,128]{2,1,0:T(1,128)} %param.15) | copy-start | bytes 1540
  53.4 48.7 %copy-start.7 = (s32[1,1,128]{2,1,0:T(1,128)S(1)}, s32[1,1,128]{2,1,0:T(1,128)}, u32[]{:S(2)}) copy-start(s32[1,1,128]{2,1,0:T(1,128)} %param.16) | copy-start | bytes 1540
  56.1 28.2 %all-to-all-start.1 = ((bf16[16,128,128]{2,1,0:T(8,128)(2,1)}), bf16[16,128,128]{2,1,0:T(8,128)(2,1)S(1)}, u32[]{:S(2)}, u32[]{:S(2)}) async-start(bf16[16,128,128]{2,1,0:T(8,128)(2,1)} %forward_sweep.1), calls=%async_computation.1 | async-start | bytes 1048576 | tf_op jit(solution)/shard_map/all_to_all | solution.py:205
  102.1 2.2 %copy-start.1 = (bf16[1,1,128,128,128]{4,3,2,1,0:T(8,128)(2,1)S(1)}, bf16[1,1,128,128,128]{4,3,2,1,0:T(8,128)(2,1)}, u32[]{:S(2)}) copy-start(bf16[1,1,128,128,128]{4,3,2,1,0:T(8,128)(2,1)} %param.14) | copy-start | bytes 12582916
  106.5 15.3 %collective-permute-start.1 = (bf16[2080,128]{1,0:T(8,128)(2,1)S(1)}, bf16[2080,128]{1,0:T(8,128)(2,1)S(1)}, u32[]{:S(2)}, u32[]{:S(2)}) collective-permute-start(bf16[2080,128]{1,0:T(8,128)(2,1)S(1)} %get-tuple-element.12), channel_id=1, source_target_pairs={{0,256},{256,0},{1,257},{257,1},{2,258},{258,2},{3,259},{259,3},{4... | collective-permute-start | bytes 1597448 | tf_op jit(solution)/shard_map/ppermute | solution.py:230

commit v2 on v1

v2 whole, which is shorter than its diff:
```python
import jax
import jax.numpy as jnp
from jax import lax
from jax.experimental import pallas as pl
from jax.experimental.pallas import tpu as pltpu
from jax.sharding import Mesh
from jax.sharding import PartitionSpec as P

F32 = jnp.float32
BF16 = jnp.bfloat16
Z = ("zh", "zl")
ROW = ("xl",) + Z
CHIP = ("xh", "y")
COL = CHIP + ("core",)
AXES = ROW + COL
SIZES = (2, 4, 4, 2, 4, 2)

E = 128
WIDE = 256
SLOTS = 128
GROUP = 16
CHUNKS = SLOTS // GROUP
NZ, NX, NC = 16, 2, 16
NR = NX * NZ
GW = 32
PACK = E + 2 * GW
NCHIP = 8

ANY = pl.BlockSpec(memory_space=pl.ANY)
VMEM = pl.BlockSpec(memory_space=pltpu.VMEM)
SMEM = pl.BlockSpec(memory_space=pltpu.SMEM)
PARAMS = pltpu.CompilerParams(vmem_limit_bytes=16 * 1024 * 1024)
CLASS = 8
HALF = CLASS // 2


def split(x):
    high = x.astype(BF16)
    return high, (x - high.astype(F32)).astype(BF16)


def pack_weight_grad(piece):
    flat = jnp.concatenate([piece[:, :E], piece[:, E:]], axis=0)
    high, low = split(flat)
    return jnp.concatenate([high, low], axis=0)


def unpack_weight_grad(packed):
    wide = packed.astype(F32)
    return wide[:16] + wide[16:]


def preload_kernel(tiles, held, sems):
    copies = [pltpu.make_async_copy(tiles.at[c], held.at[c], sems.at[c]) for c in range(CHUNKS)]
    for copy in copies:
        copy.start()
    for copy in copies:
        copy.wait()


def sweep(count, product, add):
    def chunk_step(c, carry):
        left = count - c * GROUP

        @pl.when(left >= GROUP)
        def _():
            for u0 in range(0, GROUP, 4):
                values = [product(c, u, c * GROUP + u) for u in range(u0, u0 + 4)]
                for k, value in enumerate(values):
                    add(c * GROUP + u0 + k, value)

        @pl.when(left < GROUP)
        def _():
            def one(u, inner):
                add(c * GROUP + u, product(c, u, c * GROUP + u))
                return inner

            lax.fori_loop(0, left, one, 0)

        return carry

    lax.fori_loop(0, (count + GROUP - 1) // GROUP, chunk_step, 0)


def chip_first(row, core):
    return jnp.bitwise_xor(jnp.bitwise_and(row, 1), core) * NCHIP + lax.shift_right_logical(row, 1)


def forward_kernel(count, rows, places, core, tiles, mine, peer, near, far, source, total, sems):
    arrivals = [
        pltpu.make_async_copy(mine, source.at[pl.ds(0, NZ)], sems.at[0]),
        pltpu.make_async_copy(peer, source.at[pl.ds(NZ, NZ)], sems.at[1]),
    ]
    for copy in arrivals:
        copy.start()
    total[...] = jnp.zeros_like(total)
    for copy in arrivals:
        copy.wait()

    def product(c, u, t):
        return jnp.dot(tiles[c, u], source[places[t]], preferred_element_type=F32)

    def add(t, value):
        total[chip_first(rows[t], core[0])] += value

    sweep(count[0], product, add)
    near[...] = total[:NCHIP].astype(BF16)
    far[...] = total[NCHIP:].astype(BF16)


def chip_kernel(near, far, both):
    both[...] = (near[...].astype(F32) + far[...].astype(F32)).astype(BF16)


def node_kernel(terms, scale, bias, weight, grad_out, output, pack):
    gathered = terms[0].astype(F32)
    for k in range(1, NCHIP):
        gathered = gathered + terms[k].astype(F32)
    high, low = split(gathered)
    w = weight[...]
    summed = jnp.dot(high, w, preferred_element_type=F32) + jnp.dot(low, w, preferred_element_type=F32)
    square = jnp.broadcast_to(scale[...], (E, E)).T
    r = jnp.concatenate([square, square], axis=1)
    hidden = r * summed + bias[...]
    s = jax.nn.sigmoid(hidden)
    output[...] = (hidden * s).astype(BF16)
    d_hidden = grad_out[...].astype(F32) * s * (1.0 + hidden * (1.0 - s))
    scaled = (r * d_hidden).astype(BF16)
    back = lax.dot_general(w, scaled, (((1,), (1,)), ((), ())), preferred_element_type=F32).astype(BF16)
    first = (((0,), (0,)), ((), ()))
    grad = lax.dot_general(high, scaled, first, preferred_element_type=F32)
    grad = grad + lax.dot_general(low, scaled, first, preferred_element_type=F32)
    for k in range(NCHIP):
        pack[k, pl.ds(0, E)] = back
        for c in range(2):
            first_row = 16 * k + 8 * c
            pack[k, pl.ds(E + GW * c, GW)] = pack_weight_grad(grad[first_row : first_row + 8])


def backward_kernel(count, rows, places, core, tiles, packed, keep, up, down, up2, down2, total):
    total[...] = jnp.zeros_like(total)

    def product(c, u, t):
        block = chip_first(rows[t], 0)
        return jnp.dot(packed[block, pl.ds(0, E)], tiles[c, u], preferred_element_type=F32)

    def add(t, value):
        total[places[t]] += value

    sweep(count[0], product, add)
    own = pl.ds(pl.multiple_of(E + GW * core[0], GW), GW)
    grad = unpack_weight_grad(packed[0, own])
    for k in range(1, NC):
        grad = grad + unpack_weight_grad(packed[k, own])
    high, low = split(grad)
    for ref, first, size, tail in (
        (keep, 0, CLASS, True),
        (up, CLASS, CLASS, True),
        (up2, 2 * CLASS, HALF, True),
        (down2, 2 * CLASS + HALF, HALF, False),
        (down, 3 * CLASS, CLASS, True),
    ):
        for k in range(size):
            ref[pl.ds(k * E, E)] = total[first + k].astype(BF16)
        if tail:
            ref[pl.ds(size * E, 16)] = high
            ref[pl.ds(size * E + 16, 16)] = low


def class_kernel(keep, up, down, up2, down2, pack):
    for k in range(CLASS):
        rows = pl.ds(k * E, E)
        value = keep[rows].astype(F32) + up[rows].astype(F32) + down[rows].astype(F32)
        if k < HALF:
            value = value + up2[rows].astype(F32)
        else:
            value = value + down2[pl.ds((k - HALF) * E, E)].astype(F32)
        pack[k // 2, pl.ds((k % 2) * E, E)] = value.astype(BF16)
    tail = pl.ds(CLASS * E, GW)
    grad = unpack_weight_grad(keep[tail]) + unpack_weight_grad(up[tail])
    grad = grad + unpack_weight_grad(down[tail]) + unpack_weight_grad(up2[pl.ds(HALF * E, GW)])
    high, low = split(grad)
    for h in range(4):
        pack[h, pl.ds(2 * E, 16)] = high
        pack[h, pl.ds(2 * E + 16, 16)] = low


def column_kernel(terms, mine, other, grad_piece):
    value = terms[0].astype(F32)
    for h in range(1, 4):
        value = value + terms[h].astype(F32)
    mine[...] = value[:E]
    other[...] = value[E : 2 * E]
    both = value[2 * E : 2 * E + 16] + value[2 * E + 16 : 2 * E + 32]
    piece = jnp.concatenate([both[:8], both[8:]], axis=1)
    for k in range(NX * NCHIP):
        grad_piece[pl.ds(8 * k, 8)] = piece


def last_kernel(mine, came, pieces, grad_features, grad_weight):
    grad_features[...] = (mine[...] + came[...]).T.astype(BF16)
    for c in range(2):
        for k in range(NCHIP):
            first = 8 * (NX * NCHIP * c + k)
            piece = pieces[pl.ds(first, 8)] + pieces[pl.ds(first + 8 * NCHIP, 8)]
            grad_weight[pl.ds(16 * k + 8 * c, 8)] = piece


def shape(dims, kind=BF16):
    return jax.ShapeDtypeStruct(dims, kind)


def on_device(features, grad_out, row_scale, out_bias, weight, tile_vals, tile_rows, tile_cols, tile_count):
    rows = tile_rows.reshape(SLOTS)
    cols = tile_cols.reshape(SLOTS)
    count = tile_count.reshape(1)
    core = lax.axis_index("core").astype(jnp.int32).reshape(1)
    swap = [(0, 1), (1, 0)]

    def up_z(x, step):
        return lax.ppermute(x, Z, [(k, (k + step) % NZ) for k in range(NZ)])

    flipped = jnp.bitwise_xor(cols // NZ, lax.axis_index("xl"))
    residue = jnp.mod(cols - lax.axis_index("zl"), 4)
    places = (residue * CLASS + (cols // 4) % 4 * 2 + flipped).astype(jnp.int32)
    sources = (flipped * NZ + cols % NZ).astype(jnp.int32)

    near = lax.all_gather(features, Z, axis=0, tiled=True).reshape(NZ, E, E)
    peer = lax.ppermute(near, "xl", swap)
    stored, _ = lax.optimization_barrier((tile_vals.reshape(CHUNKS, GROUP, E, E), near))
    tiles = pl.pallas_call(
        preload_kernel,
        out_shape=pltpu.VMEM((CHUNKS, GROUP, E, E), BF16),
        in_specs=[ANY],
        out_specs=VMEM,
        scratch_shapes=[pltpu.SemaphoreType.DMA((CHUNKS,))],
        compiler_params=PARAMS,
        cost_estimate=pl.CostEstimate(flops=0, bytes_accessed=8 * 1024 * 1024, transcendentals=0),
        name="preload",
    )(stored)
    half = shape((NCHIP, E, E))
    mine, far = pl.pallas_call(
        forward_kernel,
        out_shape=(half, half),
        in_specs=[SMEM] * 4 + [VMEM] + [ANY] * 2,
        out_specs=(VMEM, VMEM),
        scratch_shapes=[
            pltpu.VMEM((NR, E, E), BF16),
            pltpu.VMEM((NC, E, E), F32),
            pltpu.SemaphoreType.DMA((2,)),
        ],
        compiler_params=PARAMS,
        name="forward_sweep",
    )(count, rows, sources, core, tiles, near, peer)
    came = lax.ppermute(far, "core", swap)
    partial = pl.pallas_call(
        chip_kernel,
        out_shape=half,
        in_specs=[VMEM] * 2,
        out_specs=VMEM,
        compiler_params=PARAMS,
        name="chip_sum",
    )(mine, came)
    terms = lax.all_to_all(partial, CHIP, 0, 0, tiled=True)
    output, pack = pl.pallas_call(
        node_kernel,
        out_shape=(shape((E, WIDE)), shape((NCHIP, PACK, E))),
        in_specs=[VMEM] * 5,
        out_specs=(VMEM, VMEM),
        compiler_params=PARAMS,
        name="node_update",
    )(terms, row_scale.reshape(1, E), out_bias.reshape(1, WIDE), weight, grad_out)
    packed = lax.all_to_all(pack, CHIP, 0, 0, tiled=True)
    packed = lax.all_gather(packed, "core", axis=0, tiled=True)

    def line(blocks, tail=GW):
        return shape((blocks * E + tail, E))

    keep, up, down, up2, down2 = pl.pallas_call(
        backward_kernel,
        out_shape=(line(CLASS), line(CLASS), line(CLASS), line(HALF), line(HALF, 0)),
        in_specs=[SMEM] * 4 + [VMEM] * 2,
        out_specs=(VMEM,) * 5,
        scratch_shapes=[pltpu.VMEM((NR, E, E), F32)],
        compiler_params=PARAMS,
        name="backward_sweep",
    )(count, rows, places, core, tiles, packed)
    arrived = [up_z(up, 1), up_z(down, -1), up_z(up2, 2), up_z(down2, -2)]
    classes = pl.pallas_call(
        class_kernel,
        out_shape=shape((4, 2 * E + GW, E)),
        in_specs=[VMEM] * 5,
        out_specs=VMEM,
        compiler_params=PARAMS,
        name="class_sum",
    )(keep, *arrived)
    column = lax.all_to_all(classes, "zh", 0, 0, tiled=True)
    mine, other, piece = pl.pallas_call(
        column_kernel,
        out_shape=(shape((E, E), F32), shape((E, E), F32), shape((NX * NCHIP * 8, WIDE), F32)),
        in_specs=[VMEM],
        out_specs=(VMEM,) * 3,
        compiler_params=PARAMS,
        name="column_sum",
    )(column)
    came = lax.ppermute(other, "xl", swap)
    grads = lax.all_to_all(piece, ("xl",) + CHIP, 0, 0, tiled=True)
    grads = lax.all_gather(grads, "core", axis=0, tiled=True)
    grad_features, grad_weight = pl.pallas_call(
        last_kernel,
        out_shape=(shape((E, E)), shape((E, WIDE), F32)),
        in_specs=[VMEM] * 3,
        out_specs=(VMEM, VMEM),
        compiler_params=PARAMS,
        name="last_sum",
    )(mine, came, grads)
    return output, grad_features, grad_weight


def solution(mesh):
    fine = Mesh(mesh.devices.reshape(SIZES), AXES)
    by_row = ROW + COL
    by_col = COL + ROW
    return jax.shard_map(
        on_device,
        mesh=fine,
        in_specs=(
            P(by_col, None),
            P(by_row, None),
            P(by_row),
            P(),
            P(),
            P(ROW, COL, None, None, None),
            P(ROW, COL, None),
            P(ROW, COL, None),
            P(ROW, COL),
        ),
        out_specs=(P(by_row, None), P(by_col, None), P()),
        check_vma=False,
    )
```

time: 184 us -> 156 us (0.85)
  blocking collectives: 115 us -> 93 us
  waiting for transfers between devices: 28.6 us -> 12.9 us
  starting transfers between devices: 24 us -> 36.7 us
  local copies, waits for them, and re-layouts: 7.38 us -> 2.48 us
    all_to_all x4 -> x3, blocking collectives: 115 us -> 50.5 us  [the longest x1 25.4 us: on_device(): column = lax.all_to_all(classes, 'zh', 0, 0, tiled=True)]
    all_gather x0 -> x3, blocking collectives: none -> 42.5 us  [the longest x1 32.1 us: on_device(): near = lax.all_gather(features, Z, axis=0, tiled=True).reshape(NZ, E, E)]
    ppermute x2 -> x7, starting transfers between devices: 7.16 us -> 31.5 us  [the longest x4 13.9 us: up_z(): return lax.ppermute(x, Z, [(k, (k + step) % NZ) for k in range(NZ)])]
    all_to_all x1, starting transfers between devices: 16.9 us -> 5.16 us  [on_device(): grads = lax.all_to_all(piece, ('xl',) + CHIP, 0, 0, tiled=True)]
    ppermute x2 -> x7, waiting for transfers between devices: 17.4 us -> 9.44 us  [the longest x4 5.06 us: up_z(): return lax.ppermute(x, Z, [(k, (k + step) % NZ) for k in range(NZ)])]
    all_to_all x1, waiting for transfers between devices: 11.2 us -> 3.5 us  [on_device(): grads = lax.all_to_all(piece, ('xl',) + CHIP, 0, 0, tiled=True)]
    unnamed x21 -> x14, local copies, waits for them, and re-layouts: 6.37 us -> 2.48 us
    pallas_call x5 -> x8, Pallas kernels: 6.79 us -> 8.48 us  [the longest x1 2.84 us: on_device(): pl.pallas_call(forward_kernel, out_shape=(half, half), in_specs=[SMEM] *...]
  transfers between devices with their start and end apart: 3 -> 8, of which waited for: 3 -> 4; matrix products, arithmetic and copies ran while one was open for 0% -> 0% of each run, Pallas kernels for 0% -> 0%
where the time goes in v2:
time: 156 us; the launch traced here: 155 us
  blocking collectives  93 us (60%)
  starting transfers between devices  36.7 us (24%)
  waiting for transfers between devices  12.9 us (8%)
  Pallas kernels  8.48 us (5%)
  local copies, waits for them, and re-layouts  2.48 us (2%)
    all_gather x1, blocking collectives, on_device(): near = lax.all_gather(features, Z, axis=0, tiled=True).reshape(NZ, E, E)  32.1 us
    all_to_all x1, blocking collectives, on_device(): column = lax.all_to_all(classes, 'zh', 0, 0, tiled=True)  25.4 us
    ppermute x4, starting transfers between devices, up_z(): return lax.ppermute(x, Z, [(k, (k + step) % NZ) for k in range(NZ)])  13.9 us
    all_to_all x1, blocking collectives, on_device(): terms = lax.all_to_all(partial, CHIP, 0, 0, tiled=True)  13.5 us
    all_to_all x1, blocking collectives, on_device(): packed = lax.all_to_all(pack, CHIP, 0, 0, tiled=True)  11.6 us
    ppermute x1, starting transfers between devices, on_device(): came = lax.ppermute(far, 'core', swap)  11.3 us
    all_gather x1, blocking collectives, on_device(): grads = lax.all_gather(grads, 'core', axis=0, tiled=True)  5.63 us
    all_to_all x1, starting transfers between devices, on_device(): grads = lax.all_to_all(piece, ('xl',) + CHIP, 0, 0, tiled=True)  5.16 us
  transfers between devices with their start and end apart: 8, of which 4 were waited for; matrix products, arithmetic and copies ran while one was open for 0% of the time, Pallas kernels for 0%

profile of v2, /device:TPU:1, one launch (start us, length us, event | category | flops | bytes accessed | tf_op | source)
XLA Modules:
  0.0 155.1 jit_solution(7832126953922653115)
XLA Ops:
  0.6 32.1 %all_gather.9 = bf16[2048,128]{1,0:T(8,128)(2,1)S(1)} all-gather(bf16[128,128]{1,0:T(8,128)(2,1)} %param.9), channel_id=1, replica_groups=mesh['xl'=2,'zh'=4,'zl'=4,'xh'=2,'y'=4,'core'=2] {'zh','zl'}, dimensions={0}, use_global_device_ids=true | all-gather | bytes 557056 | tf_op jit(solution)/shard_map/all_gather | solution.py:228
  32.7 3.1 %collective-permute-start = (bf16[16,128,128]{2,1,0:T(8,128)(2,1)S(1)}, bf16[16,128,128]{2,1,0:T(8,128)(2,1)S(1)}, u32[]{:S(2)}, u32[]{:S(2)}) collective-permute-start(bf16[16,128,128]{2,1,0:T(8,128)(2,1)S(1)} %bitcast.42), channel_id=1, source_target_pairs={{0,256},{256,0},{1,257},{257,1},{2,258},{258,2},{3,259},{259,3},{4... | collective-permute-start | bytes 1572872 | tf_op jit(solution)/shard_map/ppermute | solution.py:229
  36.5 0.0 copy-start
  36.5 2.2 %copy-done = bf16[1,1,128,128,128]{4,3,2,1,0:T(8,128)(2,1)S(1)} copy-done((bf16[1,1,128,128,128]{4,3,2,1,0:T(8,128)(2,1)S(1)}, bf16[1,1,128,128,128]{4,3,2,1,0:T(8,128)(2,1)}, u32[]{:S(2)}) %copy-start) | copy-done | bytes 4194328
  38.7 0.0 copy-start.6
  38.7 0.0 copy-start.3
  38.7 0.4 preload.1.tiles
  39.0 0.3 copy-done.6
  39.3 0.0 copy-start.1
  39.3 0.0 copy-start.2
  39.3 0.0 copy-start.4
  39.3 0.0 copy-start.5
  39.4 3.2 %collective-permute-done.peer = bf16[16,128,128]{2,1,0:T(8,128)(2,1)S(1)} collective-permute-done((bf16[16,128,128]{2,1,0:T(8,128)(2,1)S(1)}, bf16[16,128,128]{2,1,0:T(8,128)(2,1)S(1)}, u32[]{:S(2)}, u32[]{:S(2)}) %collective-permute-start) | collective-permute-done | bytes 524320 | tf_op jit(solution)/shard_map/ppermute | solution.py:229
  42.6 0.0 copy-done.3
  42.6 2.8 %forward_sweep.1 = (bf16[8,128,128]{2,1,0:T(8,128)(2,1)S(1)}, bf16[8,128,128]{2,1,0:T(8,128)(2,1)S(1)}) custom-call(s32[1]{0:T(128)} %bitcast.39.count, s32[128]{0:T(128)S(1)} %bitcast.44, s32[128]{0:T(128)S(1)} %fusion.places, s32[1]{0:T(128)} %bitcast.3.core, bf16[8,16,128,128]{3,2,1,0:T(8,128)(2,1)S(1)} %preload.1.tiles, ...), custom_call_target="tpu_custom_call" | custom-call | tf_op jit(solution)/shard_map/forward_sweep/pallas_call | solution.py:242
  45.5 11.3 %collective-permute-start.1 = (bf16[8,128,128]{2,1,0:T(8,128)(2,1)S(1)}, bf16[8,128,128]{2,1,0:T(8,128)(2,1)S(1)}, u32[]{:S(2)}, u32[]{:S(2)}) collective-permute-start(bf16[8,128,128]{2,1,0:T(8,128)(2,1)S(1)} %get-tuple-element.20), channel_id=1, source_target_pairs={{0,1},{1,0},{2,3},{3,2},{4,5},{5,4},{6,7},{7,6},{8,9},{9,8},{10,11... | collective-permute-start | bytes 786440 | tf_op jit(solution)/shard_map/ppermute | solution.py:255
  56.7 1.1 collective-permute-done.1.far
  57.9 0.1 chip_sum.1
  58.0 13.5 %all_to_all.27.terms = bf16[8,128,128]{2,1,0:T(8,128)(2,1)S(1)} all-to-all(bf16[8,128,128]{2,1,0:T(8,128)(2,1)S(1)} %chip_sum.1), channel_id=1, replica_groups=mesh['xl'=2,'zh'=4,'zl'=4,'xh'=2,'y'=4,'core'=2] {'xh','y'}, dimensions={0} | all-to-all | bytes 524288 | tf_op jit(solution)/shard_map/all_to_all | solution.py:264
  71.5 0.0 copy-done.1
  71.5 0.0 copy-done.2
  71.5 0.0 copy-done.4
  71.5 0.0 copy-done.5
  71.5 0.9 node_update.1
  72.4 11.6 %all_to_all.28 = bf16[8,192,128]{2,1,0:T(8,128)(2,1)S(1)} all-to-all(bf16[8,192,128]{2,1,0:T(8,128)(2,1)S(1)} %get-tuple-element.22), channel_id=1, replica_groups=mesh['xl'=2,'zh'=4,'zl'=4,'xh'=2,'y'=4,'core'=2] {'xh','y'}, dimensions={0} | all-to-all | bytes 786432 | tf_op jit(solution)/shard_map/all_to_all | solution.py:273
  84.0 4.8 %all_gather.10.packed = bf16[16,192,128]{2,1,0:T(8,128)(2,1)S(1)} all-gather(bf16[8,192,128]{2,1,0:T(8,128)(2,1)S(1)} %all_to_all.28), channel_id=1, replica_groups=mesh['xl'=2,'zh'=4,'zl'=4,'xh'=2,'y'=4,'core'=2] {'core'}, dimensions={0}, use_global_device_ids=true | all-gather | bytes 1179648 | tf_op jit(solution)/shard_map/all_gather | solution.py:274
  88.8 2.8 %backward_sweep.1 = (bf16[1056,128]{1,0:T(8,128)(2,1)S(1)}, bf16[1056,128]{1,0:T(8,128)(2,1)S(1)}, bf16[1056,128]{1,0:T(8,128)(2,1)S(1)}, bf16[544,128]{1,0:T(8,128)(2,1)S(1)}, bf16[512,128]{1,0:T(8,128)(2,1)S(1)}) custom-call(s32[1]{0:T(128)} %bitcast.40.count, s32[128]{0:T(128)S(1)} %bitcast.45, s32[128]{0:T(128)S(1)} %get-tuple-element.33.places, ...), custom_call_target="tpu_custom_call" | custom-call | tf_op jit(solution)/shard_map/backward_sweep/pallas_call | solution.py:279
  91.6 2.5 %collective-permute-start.2 = (bf16[1056,128]{1,0:T(8,128)(2,1)S(1)}, bf16[1056,128]{1,0:T(8,128)(2,1)S(1)}, u32[]{:S(2)}, u32[]{:S(2)}) collective-permute-start(bf16[1056,128]{1,0:T(8,128)(2,1)S(1)} %get-tuple-element.24), channel_id=1, source_target_pairs={{0,16},{16,32},{32,48},{48,64},{64,80},{80,96},{96,112},{112,128},... | collective-permute-start | bytes 811016 | tf_op jit(solution)/shard_map/ppermute | solution.py:221
  94.1 4.0 %collective-permute-start.3 = (bf16[1056,128]{1,0:T(8,128)(2,1)S(1)}, bf16[1056,128]{1,0:T(8,128)(2,1)S(1)}, u32[]{:S(2)}, u32[]{:S(2)}) collective-permute-start(bf16[1056,128]{1,0:T(8,128)(2,1)S(1)} %get-tuple-element.25), channel_id=1, source_target_pairs={{0,240},{16,0},{32,16},{48,32},{64,48},{80,64},{96,80},{112,96},{1... | collective-permute-start | bytes 811016 | tf_op jit(solution)/shard_map/ppermute | solution.py:221
  98.1 1.9 %collective-permute-start.4 = (bf16[544,128]{1,0:T(8,128)(2,1)S(1)}, bf16[544,128]{1,0:T(8,128)(2,1)S(1)}, u32[]{:S(2)}, u32[]{:S(2)}) collective-permute-start(bf16[544,128]{1,0:T(8,128)(2,1)S(1)} %get-tuple-element.26), channel_id=1, source_target_pairs={{0,32},{16,48},{32,64},{48,80},{64,96},{80,112},{96,128},{112,144}... | collective-permute-start | bytes 417800 | tf_op jit(solution)/shard_map/ppermute | solution.py:221
  100.0 5.5 %collective-permute-start.5 = (bf16[512,128]{1,0:T(8,128)(2,1)S(1)}, bf16[512,128]{1,0:T(8,128)(2,1)S(1)}, u32[]{:S(2)}, u32[]{:S(2)}) collective-permute-start(bf16[512,128]{1,0:T(8,128)(2,1)S(1)} %get-tuple-element.27), channel_id=1, source_target_pairs={{0,224},{16,240},{32,0},{48,16},{64,32},{80,48},{96,64},{112,80},{... | collective-permute-start | bytes 393224 | tf_op jit(solution)/shard_map/ppermute | solution.py:221
  105.5 5.0 %collective-permute-done.5.down2 = bf16[512,128]{1,0:T(8,128)(2,1)S(1)} collective-permute-done((bf16[512,128]{1,0:T(8,128)(2,1)S(1)}, bf16[512,128]{1,0:T(8,128)(2,1)S(1)}, u32[]{:S(2)}, u32[]{:S(2)}) %collective-permute-start.5) | collective-permute-done | bytes 131104 | tf_op jit(solution)/shard_map/ppermute | solution.py:221
  110.6 0.0 collective-permute-done.4.up2
  110.6 0.0 collective-permute-done.2.up
  110.6 0.0 collective-permute-done.3.down
  110.6 0.1 class_sum.1
  110.7 25.4 %all_to_all.29.terms = bf16[4,288,128]{2,1,0:T(8,128)(2,1)S(1)} all-to-all(bf16[4,288,128]{2,1,0:T(8,128)(2,1)S(1)} %class_sum.1), channel_id=1, replica_groups=mesh['xl'=2,'zh'=4,'zl'=4,'xh'=2,'y'=4,'core'=2] {'zh'}, dimensions={0} | all-to-all | bytes 589824 | tf_op jit(solution)/shard_map/all_to_all | solution.py:297
  136.1 0.7 column_sum.1
  136.8 5.2 %all-to-all-start.3 = ((f32[16,8,256]{2,1,0:T(8,128)}), f32[16,8,256]{2,1,0:T(8,128)S(1)}, u32[]{:S(2)}, u32[]{:S(2)}) async-start(f32[16,8,256]{2,1,0:T(8,128)} %bitcast.8), calls=%async_computation.3 | async-start | bytes 262144 | tf_op jit(solution)/shard_map/all_to_all | solution.py:307
  141.9 3.3 %collective-permute-start.6 = (f32[128,128]{1,0:T(8,128)S(1)}, f32[128,128]{1,0:T(8,128)S(1)}, u32[]{:S(2)}, u32[]{:S(2)}) collective-permute-start(f32[128,128]{1,0:T(8,128)S(1)} %get-tuple-element.29), channel_id=1, source_target_pairs={{0,256},{256,0},{1,257},{257,1},{2,258},{258,2},{3,259},{259,3},{4... | collective-permute-start | bytes 196616 | tf_op jit(solution)/shard_map/ppermute | solution.py:306
  145.2 3.5 %all-to-all-done.3 = f32[16,8,256]{2,1,0:T(8,128)S(1)} async-done(((f32[16,8,256]{2,1,0:T(8,128)}), f32[16,8,256]{2,1,0:T(8,128)S(1)}, u32[]{:S(2)}, u32[]{:S(2)}) %all-to-all-start.3) | async-done | bytes 131104 | tf_op jit(solution)/shard_map/all_to_all | solution.py:307
  148.7 5.6 %all_gather.11.pieces = f32[256,256]{1,0:T(8,128)S(1)} all-gather(f32[128,256]{1,0:T(8,128)S(1)} %bitcast.48), channel_id=1, replica_groups=mesh['xl'=2,'zh'=4,'zl'=4,'xh'=2,'y'=4,'core'=2] {'core'}, dimensions={0}, use_global_device_ids=true | all-gather | bytes 393216 | tf_op jit(solution)/shard_map/all_gather | solution.py:308
  154.3 0.0 collective-permute-done.6.came
  154.3 0.7 last_sum.1
  (2 shorter events, 0.0 us)
Async XLA Ops:
  32.7 9.9 %collective-permute-start = (bf16[16,128,128]{2,1,0:T(8,128)(2,1)S(1)}, bf16[16,128,128]{2,1,0:T(8,128)(2,1)S(1)}, u32[]{:S(2)}, u32[]{:S(2)}) collective-permute-start(bf16[16,128,128]{2,1,0:T(8,128)(2,1)S(1)} %bitcast.42), channel_id=1, source_target_pairs={{0,256},{256,0},{1,257},{257,1},{2,258},{258,2},{3,259},{259,3},{4... | collective-permute-start | bytes 1572872 | tf_op jit(solution)/shard_map/ppermute | solution.py:229
  36.5 2.2 %copy-start = (bf16[1,1,128,128,128]{4,3,2,1,0:T(8,128)(2,1)S(1)}, bf16[1,1,128,128,128]{4,3,2,1,0:T(8,128)(2,1)}, u32[]{:S(2)}) copy-start(bf16[1,1,128,128,128]{4,3,2,1,0:T(8,128)(2,1)} %param.14) | copy-start | bytes 12582916
  38.7 0.7 copy-start.6
  38.7 4.0 %copy-start.3 = (s32[1,1,128]{2,1,0:T(1,128)S(1)}, s32[1,1,128]{2,1,0:T(1,128)}, u32[]{:S(2)}) copy-start(s32[1,1,128]{2,1,0:T(1,128)} %param.15) | copy-start | bytes 1540
  39.3 32.2 %copy-start.1 = (bf16[128,256]{1,0:T(8,128)(2,1)S(1)}, bf16[128,256]{1,0:T(8,128)(2,1)}, u32[]{:S(2)}) copy-start(bf16[128,256]{1,0:T(8,128)(2,1)} %weight.1) | copy-start | bytes 196612
  39.3 32.2 %copy-start.2 = (bf16[128,256]{1,0:T(8,128)(2,1)S(1)}, bf16[128,256]{1,0:T(8,128)(2,1)}, u32[]{:S(2)}) copy-start(bf16[128,256]{1,0:T(8,128)(2,1)} %grad_out.1) | copy-start | bytes 196612
  39.3 32.2 %copy-start.4 = (f32[256]{0:T(256)S(1)}, f32[256]{0:T(256)}, u32[]{:S(2)}) copy-start(f32[256]{0:T(256)} %param.12) | copy-start | bytes 3076
  39.3 32.2 %copy-start.5 = (f32[128]{0:T(128)S(1)}, f32[128]{0:T(128)}, u32[]{:S(2)}) copy-start(f32[128]{0:T(128)} %param.11) | copy-start | bytes 1540
  45.5 12.4 %collective-permute-start.1 = (bf16[8,128,128]{2,1,0:T(8,128)(2,1)S(1)}, bf16[8,128,128]{2,1,0:T(8,128)(2,1)S(1)}, u32[]{:S(2)}, u32[]{:S(2)}) collective-permute-start(bf16[8,128,128]{2,1,0:T(8,128)(2,1)S(1)} %get-tuple-element.20), channel_id=1, source_target_pairs={{0,1},{1,0},{2,3},{3,2},{4,5},{5,4},{6,7},{7,6},{8,9},{9,8},{10,11... | collective-permute-start | bytes 786440 | tf_op jit(solution)/shard_map/ppermute | solution.py:255
  91.6 19.0 %collective-permute-start.2 = (bf16[1056,128]{1,0:T(8,128)(2,1)S(1)}, bf16[1056,128]{1,0:T(8,128)(2,1)S(1)}, u32[]{:S(2)}, u32[]{:S(2)}) collective-permute-start(bf16[1056,128]{1,0:T(8,128)(2,1)S(1)} %get-tuple-element.24), channel_id=1, source_target_pairs={{0,16},{16,32},{32,48},{48,64},{64,80},{80,96},{96,112},{112,128},... | collective-permute-start | bytes 811016 | tf_op jit(solution)/shard_map/ppermute | solution.py:221
  94.1 16.4 %collective-permute-start.3 = (bf16[1056,128]{1,0:T(8,128)(2,1)S(1)}, bf16[1056,128]{1,0:T(8,128)(2,1)S(1)}, u32[]{:S(2)}, u32[]{:S(2)}) collective-permute-start(bf16[1056,128]{1,0:T(8,128)(2,1)S(1)} %get-tuple-element.25), channel_id=1, source_target_pairs={{0,240},{16,0},{32,16},{48,32},{64,48},{80,64},{96,80},{112,96},{1... | collective-permute-start | bytes 811016 | tf_op jit(solution)/shard_map/ppermute | solution.py:221
  98.1 12.5 %collective-permute-start.4 = (bf16[544,128]{1,0:T(8,128)(2,1)S(1)}, bf16[544,128]{1,0:T(8,128)(2,1)S(1)}, u32[]{:S(2)}, u32[]{:S(2)}) collective-permute-start(bf16[544,128]{1,0:T(8,128)(2,1)S(1)} %get-tuple-element.26), channel_id=1, source_target_pairs={{0,32},{16,48},{32,64},{48,80},{64,96},{80,112},{96,128},{112,144}... | collective-permute-start | bytes 417800 | tf_op jit(solution)/shard_map/ppermute | solution.py:221
  100.0 10.5 %collective-permute-start.5 = (bf16[512,128]{1,0:T(8,128)(2,1)S(1)}, bf16[512,128]{1,0:T(8,128)(2,1)S(1)}, u32[]{:S(2)}, u32[]{:S(2)}) collective-permute-start(bf16[512,128]{1,0:T(8,128)(2,1)S(1)} %get-tuple-element.27), channel_id=1, source_target_pairs={{0,224},{16,240},{32,0},{48,16},{64,32},{80,48},{96,64},{112,80},{... | collective-permute-start | bytes 393224 | tf_op jit(solution)/shard_map/ppermute | solution.py:221
  136.8 11.9 %all-to-all-start.3 = ((f32[16,8,256]{2,1,0:T(8,128)}), f32[16,8,256]{2,1,0:T(8,128)S(1)}, u32[]{:S(2)}, u32[]{:S(2)}) async-start(f32[16,8,256]{2,1,0:T(8,128)} %bitcast.8), calls=%async_computation.3 | async-start | bytes 262144 | tf_op jit(solution)/shard_map/all_to_all | solution.py:307
  141.9 12.4 %collective-permute-start.6 = (f32[128,128]{1,0:T(8,128)S(1)}, f32[128,128]{1,0:T(8,128)S(1)}, u32[]{:S(2)}, u32[]{:S(2)}) collective-permute-start(f32[128,128]{1,0:T(8,128)S(1)} %get-tuple-element.29), channel_id=1, source_target_pairs={{0,256},{256,0},{1,257},{257,1},{2,258},{258,2},{3,259},{259,3},{4... | collective-permute-start | bytes 196616 | tf_op jit(solution)/shard_map/ppermute | solution.py:306

commit v3 on v2

v3 whole, which is shorter than its diff:
```python
import jax
import jax.numpy as jnp
from jax import lax
from jax.experimental import pallas as pl
from jax.experimental.pallas import tpu as pltpu
from jax.sharding import Mesh
from jax.sharding import PartitionSpec as P

F32 = jnp.float32
BF16 = jnp.bfloat16
Z = ("zh", "zl")
ROW = ("xl",) + Z
CHIP = ("xh", "y")
COL = CHIP + ("core",)
AXES = ROW + COL
SIZES = (2, 4, 4, 2, 4, 2)

E = 128
WIDE = 256
SLOTS = 128
GROUP = 16
CHUNKS = SLOTS // GROUP
NZ, NX, NC = 16, 2, 16
NR = NX * NZ
GW = 32
PACK = E + GW
UNROLL = 64
NCHIP = 8

ANY = pl.BlockSpec(memory_space=pl.ANY)
VMEM = pl.BlockSpec(memory_space=pltpu.VMEM)
SMEM = pl.BlockSpec(memory_space=pltpu.SMEM)
PARAMS = pltpu.CompilerParams(vmem_limit_bytes=16 * 1024 * 1024)
CLASS = 8
HALF = CLASS // 2


def split(x):
    high = x.astype(BF16)
    return high, (x - high.astype(F32)).astype(BF16)


def preload_kernel(tiles, held, sems):
    parts = [pl.ds(c * GROUP, GROUP) for c in range(CHUNKS)]
    copies = [pltpu.make_async_copy(tiles.at[p], held.at[p], sems.at[c]) for c, p in enumerate(parts)]
    for copy in copies:
        copy.start()
    for copy in copies:
        copy.wait()


def sweep(count, left, right, target, total, spare):
    def step(c, carry):
        for u in range(UNROLL):
            t = c * UNROLL + u
            place = jnp.where(t < count, target(t), spare)
            total[place] += jnp.dot(left(t), right(t), preferred_element_type=F32)
        return carry

    lax.fori_loop(0, (count + UNROLL - 1) // UNROLL, step, 0)


def chip_first(row, core):
    return jnp.bitwise_xor(jnp.bitwise_and(row, 1), core) * NCHIP + lax.shift_right_logical(row, 1)


def forward_kernel(count, rows, places, core, tiles, mine, peer, near, far, source, total, sems):
    arrivals = [
        pltpu.make_async_copy(mine, source.at[pl.ds(0, NZ)], sems.at[0]),
        pltpu.make_async_copy(peer, source.at[pl.ds(NZ, NZ)], sems.at[1]),
    ]
    for copy in arrivals:
        copy.start()
    total[...] = jnp.zeros_like(total)
    for copy in arrivals:
        copy.wait()

    sweep(
        count[0],
        lambda t: tiles[t],
        lambda t: source[places[t]],
        lambda t: chip_first(rows[t], core[0]),
        total,
        NC,
    )
    near[...] = total[:NCHIP].astype(BF16)
    far[...] = total[NCHIP:NC].astype(BF16)


def chip_kernel(near, far, both):
    both[...] = (near[...].astype(F32) + far[...].astype(F32)).astype(BF16)


def node_kernel(terms, scale, bias, weight, grad_out, output, pack):
    gathered = terms[0].astype(F32)
    for k in range(1, NCHIP):
        gathered = gathered + terms[k].astype(F32)
    high, low = split(gathered)
    w = weight[...]
    summed = jnp.dot(high, w, preferred_element_type=F32) + jnp.dot(low, w, preferred_element_type=F32)
    square = jnp.broadcast_to(scale[...], (E, E)).T
    r = jnp.concatenate([square, square], axis=1)
    hidden = r * summed + bias[...]
    s = jax.nn.sigmoid(hidden)
    output[...] = (hidden * s).astype(BF16)
    d_hidden = grad_out[...].astype(F32) * s * (1.0 + hidden * (1.0 - s))
    scaled = (r * d_hidden).astype(BF16)
    back = lax.dot_general(w, scaled, (((1,), (1,)), ((), ())), preferred_element_type=F32).astype(BF16)
    first = (((0,), (0,)), ((), ()))
    grad = lax.dot_general(high, scaled, first, preferred_element_type=F32)
    grad = grad + lax.dot_general(low, scaled, first, preferred_element_type=F32)
    for k in range(NCHIP):
        pack[k, pl.ds(0, E)] = back
        share = grad[16 * k : 16 * k + 16]
        pack[k, pl.ds(E, 16)] = share[:, :E].astype(BF16)
        pack[k, pl.ds(E + 16, 16)] = share[:, E:].astype(BF16)


def backward_kernel(count, rows, places, tiles, packed, keep, up, down, up2, down2, total):
    total[...] = jnp.zeros_like(total)

    sweep(
        count[0],
        lambda t: packed[chip_first(rows[t], 0), pl.ds(0, E)],
        lambda t: tiles[t],
        lambda t: places[t],
        total,
        NR,
    )
    grad = packed[0, pl.ds(E, GW)].astype(F32)
    for k in range(1, NC):
        grad = grad + packed[k, pl.ds(E, GW)].astype(F32)
    sent = grad.astype(BF16)
    for ref, first, size, tail in (
        (keep, 0, CLASS, True),
        (up, CLASS, CLASS, True),
        (up2, 2 * CLASS, HALF, True),
        (down2, 2 * CLASS + HALF, HALF, False),
        (down, 3 * CLASS, CLASS, True),
    ):
        for k in range(size):
            ref[pl.ds(k * E, E)] = total[first + k].astype(BF16)
        if tail:
            ref[pl.ds(size * E, GW)] = sent


def class_kernel(keep, up, down, up2, down2, mine, other):
    for k in range(CLASS):
        rows = pl.ds(k * E, E)
        value = keep[rows].astype(F32) + up[rows].astype(F32) + down[rows].astype(F32)
        if k < HALF:
            value = value + up2[rows].astype(F32)
        else:
            value = value + down2[pl.ds((k - HALF) * E, E)].astype(F32)
        target = pl.ds(k // 2 * E, E)
        if k % 2 == 0:
            mine[target] = value
        else:
            other[target] = value.astype(BF16)
    tail = pl.ds(CLASS * E, GW)
    grad = keep[tail].astype(F32) + up[tail].astype(F32) + down[tail].astype(F32)
    grad = grad + up2[pl.ds(HALF * E, GW)].astype(F32)
    mine[pl.ds(HALF * E, GW)] = grad
    other[pl.ds(HALF * E, GW)] = grad.astype(BF16)


def pair_kernel(mine, came, pack):
    tail = pl.ds(HALF * E, GW)
    grad = (mine[tail] + came[tail].astype(F32)).astype(BF16)
    for h in range(4):
        rows = pl.ds(h * E, E)
        pack[h, pl.ds(0, E)] = (mine[rows] + came[rows].astype(F32)).astype(BF16)
        pack[h, pl.ds(E, GW)] = grad


def last_kernel(terms, grad_features, pieces):
    value = terms[0].astype(F32)
    for h in range(1, 4):
        value = value + terms[h].astype(F32)
    grad_features[...] = value[:E].T.astype(BF16)
    share = jnp.concatenate([value[E : E + 16], value[E + 16 :]], axis=1)
    for k in range(NCHIP):
        pieces[k] = share


def shape(dims, kind=BF16):
    return jax.ShapeDtypeStruct(dims, kind)


def on_device(features, grad_out, row_scale, out_bias, weight, tile_vals, tile_rows, tile_cols, tile_count):
    rows = tile_rows.reshape(SLOTS)
    cols = tile_cols.reshape(SLOTS)
    count = tile_count.reshape(1)
    core = lax.axis_index("core").astype(jnp.int32).reshape(1)
    swap = [(0, 1), (1, 0)]

    def up_z(x, step):
        return lax.ppermute(x, Z, [(k, (k + step) % NZ) for k in range(NZ)])

    flipped = jnp.bitwise_xor(cols // NZ, lax.axis_index("xl"))
    residue = jnp.mod(cols - lax.axis_index("zl"), 4)
    places = (residue * CLASS + (cols // 4) % 4 * 2 + flipped).astype(jnp.int32)
    sources = (flipped * NZ + cols % NZ).astype(jnp.int32)

    near = lax.all_gather(features, Z, axis=0, tiled=True).reshape(NZ, E, E)
    peer = lax.ppermute(near, "xl", swap)
    stored, _ = lax.optimization_barrier((tile_vals.reshape(SLOTS, E, E), near))
    tiles = pl.pallas_call(
        preload_kernel,
        out_shape=pltpu.VMEM((SLOTS, E, E), BF16),
        in_specs=[ANY],
        out_specs=VMEM,
        scratch_shapes=[pltpu.SemaphoreType.DMA((CHUNKS,))],
        compiler_params=PARAMS,
        cost_estimate=pl.CostEstimate(flops=0, bytes_accessed=8 * 1024 * 1024, transcendentals=0),
        name="preload",
    )(stored)
    half = shape((NCHIP, E, E))
    mine, far = pl.pallas_call(
        forward_kernel,
        out_shape=(half, half),
        in_specs=[SMEM] * 4 + [VMEM] + [ANY] * 2,
        out_specs=(VMEM, VMEM),
        scratch_shapes=[
            pltpu.VMEM((NR, E, E), BF16),
            pltpu.VMEM((NC + 1, E, E), F32),
            pltpu.SemaphoreType.DMA((2,)),
        ],
        compiler_params=PARAMS,
        name="forward_sweep",
    )(count, rows, sources, core, tiles, near, peer)
    came = lax.ppermute(far, "core", swap)
    partial = pl.pallas_call(
        chip_kernel,
        out_shape=half,
        in_specs=[VMEM] * 2,
        out_specs=VMEM,
        compiler_params=PARAMS,
        name="chip_sum",
    )(mine, came)
    terms = lax.all_to_all(partial, CHIP, 0, 0, tiled=True)
    output, pack = pl.pallas_call(
        node_kernel,
        out_shape=(shape((E, WIDE)), shape((NCHIP, PACK, E))),
        in_specs=[VMEM] * 5,
        out_specs=(VMEM, VMEM),
        compiler_params=PARAMS,
        name="node_update",
    )(terms, row_scale.reshape(1, E), out_bias.reshape(1, WIDE), weight, grad_out)
    packed = lax.all_to_all(pack, CHIP, 0, 0, tiled=True)
    packed = lax.all_gather(packed, "core", axis=0, tiled=True)

    def line(blocks, tail=GW):
        return shape((blocks * E + tail, E))

    keep, up, down, up2, down2 = pl.pallas_call(
        backward_kernel,
        out_shape=(line(CLASS), line(CLASS), line(CLASS), line(HALF), line(HALF, 0)),
        in_specs=[SMEM] * 3 + [VMEM] * 2,
        out_specs=(VMEM,) * 5,
        scratch_shapes=[pltpu.VMEM((NR + 1, E, E), F32)],
        compiler_params=PARAMS,
        name="backward_sweep",
    )(count, rows, places, tiles, packed)
    arrived = [up_z(up, 1), up_z(down, -1), up_z(up2, 2), up_z(down2, -2)]
    mine, other = pl.pallas_call(
        class_kernel,
        out_shape=(shape((HALF * E + GW, E), F32), line(HALF)),
        in_specs=[VMEM] * 5,
        out_specs=(VMEM, VMEM),
        compiler_params=PARAMS,
        name="class_sum",
    )(keep, *arrived)
    came = lax.ppermute(other, "xl", swap)
    pairs = pl.pallas_call(
        pair_kernel,
        out_shape=shape((4, E + GW, E)),
        in_specs=[VMEM] * 2,
        out_specs=VMEM,
        compiler_params=PARAMS,
        name="pair_sum",
    )(mine, came)
    column = lax.all_to_all(pairs, "zh", 0, 0, tiled=True)
    grad_features, pieces = pl.pallas_call(
        last_kernel,
        out_shape=(shape((E, E)), shape((NCHIP, 16, WIDE), F32)),
        in_specs=[VMEM],
        out_specs=(VMEM, VMEM),
        compiler_params=PARAMS,
        name="last_sum",
    )(column)
    grad_weight = lax.all_to_all(pieces, CHIP, 0, 0, tiled=True).reshape(E, WIDE)
    return output, grad_features, grad_weight


def solution(mesh):
    fine = Mesh(mesh.devices.reshape(SIZES), AXES)
    by_row = ROW + COL
    by_col = COL + ROW
    return jax.shard_map(
        on_device,
        mesh=fine,
        in_specs=(
            P(by_col, None),
            P(by_row, None),
            P(by_row),
            P(),
            P(),
            P(ROW, COL, None, None, None),
            P(ROW, COL, None),
            P(ROW, COL, None),
            P(ROW, COL),
        ),
        out_specs=(P(by_row, None), P(by_col, None), P()),
        check_vma=False,
    )
```

time: 156 us -> 150 us (0.962)
  the two profiles are of different devices: /device:TPU:1 before, /device:TPU:8 now
where the time goes in v3:
time: 150 us
  blocking collectives  101 us (67%)
  starting transfers between devices  22.2 us (15%)
  waiting for transfers between devices  14.4 us (10%)
  Pallas kernels  7.24 us (5%)
  local copies, waits for them, and re-layouts  3.14 us (2%)
    all_gather x1, blocking collectives, on_device(): near = lax.all_gather(features, Z, axis=0, tiled=True).reshape(NZ, E, E)  38.8 us
    all_to_all x1, blocking collectives, on_device(): column = lax.all_to_all(pairs, 'zh', 0, 0, tiled=True)  21.8 us
    ppermute x4, starting transfers between devices, up_z(): return lax.ppermute(x, Z, [(k, (k + step) % NZ) for k in range(NZ)])  15 us
    all_to_all x1, blocking collectives, on_device(): terms = lax.all_to_all(partial, CHIP, 0, 0, tiled=True)  14.4 us
    all_to_all x1, blocking collectives, on_device(): packed = lax.all_to_all(pack, CHIP, 0, 0, tiled=True)  12.2 us
    all_to_all x1, blocking collectives, on_device(): lax.all_to_all(pieces, CHIP, 0, 0, tiled=True).reshape(E, WIDE)  11.7 us
    ppermute x1, waiting for transfers between devices, on_device(): came = lax.ppermute(other, 'xl', swap)  5.02 us
    ppermute x1, waiting for transfers between devices, on_device(): peer = lax.ppermute(near, 'xl', swap)  4.11 us
  transfers between devices with their start and end apart: 7, of which 4 were waited for; matrix products, arithmetic and copies ran while one was open for 0% of the time, Pallas kernels for 0%

profile of v3, /device:TPU:8, one launch (start us, length us, event | category | flops | bytes accessed | tf_op | source)
XLA Modules:
  0.0 149.7 jit_solution(12575465455084462901)
XLA Ops:
  0.6 38.8 %all_gather.6 = bf16[2048,128]{1,0:T(8,128)(2,1)S(1)} all-gather(bf16[128,128]{1,0:T(8,128)(2,1)} %param.9), channel_id=1, replica_groups=mesh['xl'=2,'zh'=4,'zl'=4,'xh'=2,'y'=4,'core'=2] {'zh','zl'}, dimensions={0}, use_global_device_ids=true | all-gather | bytes 557056 | tf_op jit(solution)/shard_map/all_gather | solution.py:205
  39.4 3.4 %collective-permute-start = (bf16[16,128,128]{2,1,0:T(8,128)(2,1)S(1)}, bf16[16,128,128]{2,1,0:T(8,128)(2,1)S(1)}, u32[]{:S(2)}, u32[]{:S(2)}) collective-permute-start(bf16[16,128,128]{2,1,0:T(8,128)(2,1)S(1)} %bitcast.41), channel_id=1, source_target_pairs={{0,256},{256,0},{1,257},{257,1},{2,258},{258,2},{3,259},{259,3},{4... | collective-permute-start | bytes 1572872 | tf_op jit(solution)/shard_map/ppermute | solution.py:206
  43.5 0.0 copy-start
  43.5 2.2 %copy-done = bf16[1,1,128,128,128]{4,3,2,1,0:T(8,128)(2,1)S(1)} copy-done((bf16[1,1,128,128,128]{4,3,2,1,0:T(8,128)(2,1)S(1)}, bf16[1,1,128,128,128]{4,3,2,1,0:T(8,128)(2,1)}, u32[]{:S(2)}) %copy-start) | copy-done | bytes 4194328
  45.7 0.0 copy-start.6
  45.7 0.0 copy-start.3
  45.7 0.4 preload.1.tiles
  46.1 0.3 copy-done.6
  46.3 0.0 copy-start.1
  46.3 0.0 copy-start.2
  46.3 0.0 copy-start.4
  46.3 0.0 copy-start.5
  46.4 4.1 %collective-permute-done.peer = bf16[16,128,128]{2,1,0:T(8,128)(2,1)S(1)} collective-permute-done((bf16[16,128,128]{2,1,0:T(8,128)(2,1)S(1)}, bf16[16,128,128]{2,1,0:T(8,128)(2,1)S(1)}, u32[]{:S(2)}, u32[]{:S(2)}) %collective-permute-start) | collective-permute-done | bytes 524320 | tf_op jit(solution)/shard_map/ppermute | solution.py:206
  50.5 0.0 copy-done.3
  50.5 2.5 %forward_sweep.1 = (bf16[8,128,128]{2,1,0:T(8,128)(2,1)S(1)}, bf16[8,128,128]{2,1,0:T(8,128)(2,1)S(1)}) custom-call(s32[1]{0:T(128)} %bitcast.38.count, s32[128]{0:T(128)S(1)} %bitcast.43, s32[128]{0:T(128)S(1)} %fusion.places, s32[1]{0:T(128)} %bitcast.3.core, bf16[128,128,128]{2,1,0:T(8,128)(2,1)S(1)} %preload.1.tiles, bf16[16,128,128]{2,1,0:T(8,128)(2,1)S(1)} %bitcast.42, ...), custom_call_target="tpu_custom_call" | custom-call | tf_op jit(solution)/shard_map/forward_sweep/pallas_call | solution.py:219
  53.0 1.9 %collective-permute-start.1 = (bf16[8,128,128]{2,1,0:T(8,128)(2,1)S(1)}, bf16[8,128,128]{2,1,0:T(8,128)(2,1)S(1)}, u32[]{:S(2)}, u32[]{:S(2)}) collective-permute-start(bf16[8,128,128]{2,1,0:T(8,128)(2,1)S(1)} %get-tuple-element.19), channel_id=1, source_target_pairs={{0,1},{1,0},{2,3},{3,2},{4,5},{5,4},{6,7},{7,6},{8,9},{9,8},{10,11... | collective-permute-start | bytes 786440 | tf_op jit(solution)/shard_map/ppermute | solution.py:232
  55.0 1.5 %collective-permute-done.1.far = bf16[8,128,128]{2,1,0:T(8,128)(2,1)S(1)} collective-permute-done((bf16[8,128,128]{2,1,0:T(8,128)(2,1)S(1)}, bf16[8,128,128]{2,1,0:T(8,128)(2,1)S(1)}, u32[]{:S(2)}, u32[]{:S(2)}) %collective-permute-start.1) | collective-permute-done | bytes 262176 | tf_op jit(solution)/shard_map/ppermute | solution.py:232
  56.5 0.1 chip_sum.1
  56.5 14.4 %all_to_all.20.terms = bf16[8,128,128]{2,1,0:T(8,128)(2,1)S(1)} all-to-all(bf16[8,128,128]{2,1,0:T(8,128)(2,1)S(1)} %chip_sum.1), channel_id=1, replica_groups=mesh['xl'=2,'zh'=4,'zl'=4,'xh'=2,'y'=4,'core'=2] {'xh','y'}, dimensions={0} | all-to-all | bytes 524288 | tf_op jit(solution)/shard_map/all_to_all | solution.py:241
  70.9 0.0 copy-done.1
  70.9 0.0 copy-done.2
  70.9 0.0 copy-done.4
  70.9 0.0 copy-done.5
  70.9 0.9 node_update.1
  71.8 12.2 %all_to_all.21 = bf16[8,160,128]{2,1,0:T(8,128)(2,1)S(1)} all-to-all(bf16[8,160,128]{2,1,0:T(8,128)(2,1)S(1)} %get-tuple-element.21), channel_id=1, replica_groups=mesh['xl'=2,'zh'=4,'zl'=4,'xh'=2,'y'=4,'core'=2] {'xh','y'}, dimensions={0} | all-to-all | bytes 655360 | tf_op jit(solution)/shard_map/all_to_all | solution.py:250
  84.0 2.3 %all_gather.7.packed = bf16[16,160,128]{2,1,0:T(8,128)(2,1)S(1)} all-gather(bf16[8,160,128]{2,1,0:T(8,128)(2,1)S(1)} %all_to_all.21), channel_id=1, replica_groups=mesh['xl'=2,'zh'=4,'zl'=4,'xh'=2,'y'=4,'core'=2] {'core'}, dimensions={0}, use_global_device_ids=true | all-gather | bytes 983040 | tf_op jit(solution)/shard_map/all_gather | solution.py:251
  86.2 2.5 %backward_sweep.1 = (bf16[1056,128]{1,0:T(8,128)(2,1)S(1)}, bf16[1056,128]{1,0:T(8,128)(2,1)S(1)}, bf16[1056,128]{1,0:T(8,128)(2,1)S(1)}, bf16[544,128]{1,0:T(8,128)(2,1)S(1)}, bf16[512,128]{1,0:T(8,128)(2,1)S(1)}) custom-call(s32[1]{0:T(128)} %bitcast.39.count, s32[128]{0:T(128)S(1)} %bitcast.44, s32[128]{0:T(128)S(1)} %get-tuple-element.31.places, ...), custom_call_target="tpu_custom_call" | custom-call | tf_op jit(solution)/shard_map/backward_sweep/pallas_call | solution.py:256
  88.8 1.9 %collective-permute-start.2 = (bf16[1056,128]{1,0:T(8,128)(2,1)S(1)}, bf16[1056,128]{1,0:T(8,128)(2,1)S(1)}, u32[]{:S(2)}, u32[]{:S(2)}) collective-permute-start(bf16[1056,128]{1,0:T(8,128)(2,1)S(1)} %get-tuple-element.23), channel_id=1, source_target_pairs={{0,16},{16,32},{32,48},{48,64},{64,80},{80,96},{96,112},{112,128},... | collective-permute-start | bytes 811016 | tf_op jit(solution)/shard_map/ppermute | solution.py:198
  90.7 5.1 %collective-permute-start.3 = (bf16[1056,128]{1,0:T(8,128)(2,1)S(1)}, bf16[1056,128]{1,0:T(8,128)(2,1)S(1)}, u32[]{:S(2)}, u32[]{:S(2)}) collective-permute-start(bf16[1056,128]{1,0:T(8,128)(2,1)S(1)} %get-tuple-element.24), channel_id=1, source_target_pairs={{0,240},{16,0},{32,16},{48,32},{64,48},{80,64},{96,80},{112,96},{1... | collective-permute-start | bytes 811016 | tf_op jit(solution)/shard_map/ppermute | solution.py:198
  95.9 1.9 %collective-permute-start.4 = (bf16[544,128]{1,0:T(8,128)(2,1)S(1)}, bf16[544,128]{1,0:T(8,128)(2,1)S(1)}, u32[]{:S(2)}, u32[]{:S(2)}) collective-permute-start(bf16[544,128]{1,0:T(8,128)(2,1)S(1)} %get-tuple-element.25), channel_id=1, source_target_pairs={{0,32},{16,48},{32,64},{48,80},{64,96},{80,112},{96,128},{112,144}... | collective-permute-start | bytes 417800 | tf_op jit(solution)/shard_map/ppermute | solution.py:198
  97.8 6.0 %collective-permute-start.5 = (bf16[512,128]{1,0:T(8,128)(2,1)S(1)}, bf16[512,128]{1,0:T(8,128)(2,1)S(1)}, u32[]{:S(2)}, u32[]{:S(2)}) collective-permute-start(bf16[512,128]{1,0:T(8,128)(2,1)S(1)} %get-tuple-element.26), channel_id=1, source_target_pairs={{0,224},{16,240},{32,0},{48,16},{64,32},{80,48},{96,64},{112,80},{... | collective-permute-start | bytes 393224 | tf_op jit(solution)/shard_map/ppermute | solution.py:198
  103.8 3.8 %collective-permute-done.5.down2 = bf16[512,128]{1,0:T(8,128)(2,1)S(1)} collective-permute-done((bf16[512,128]{1,0:T(8,128)(2,1)S(1)}, bf16[512,128]{1,0:T(8,128)(2,1)S(1)}, u32[]{:S(2)}, u32[]{:S(2)}) %collective-permute-start.5) | collective-permute-done | bytes 131104 | tf_op jit(solution)/shard_map/ppermute | solution.py:198
  107.6 0.0 collective-permute-done.4.up2
  107.6 0.0 collective-permute-done.2.up
  107.6 0.0 collective-permute-done.3.down
  107.6 0.1 class_sum.1
  107.8 1.9 %collective-permute-start.6 = (bf16[544,128]{1,0:T(8,128)(2,1)S(1)}, bf16[544,128]{1,0:T(8,128)(2,1)S(1)}, u32[]{:S(2)}, u32[]{:S(2)}) collective-permute-start(bf16[544,128]{1,0:T(8,128)(2,1)S(1)} %get-tuple-element.28), channel_id=1, source_target_pairs={{0,256},{256,0},{1,257},{257,1},{2,258},{258,2},{3,259},{259,3},{4... | collective-permute-start | bytes 417800 | tf_op jit(solution)/shard_map/ppermute | solution.py:274
  109.7 5.0 %collective-permute-done.6.came = bf16[544,128]{1,0:T(8,128)(2,1)S(1)} collective-permute-done((bf16[544,128]{1,0:T(8,128)(2,1)S(1)}, bf16[544,128]{1,0:T(8,128)(2,1)S(1)}, u32[]{:S(2)}, u32[]{:S(2)}) %collective-permute-start.6) | collective-permute-done | bytes 139296 | tf_op jit(solution)/shard_map/ppermute | solution.py:274
  114.8 21.8 %all_to_all.22.terms = bf16[4,160,128]{2,1,0:T(8,128)(2,1)S(1)} all-to-all(bf16[4,160,128]{2,1,0:T(8,128)(2,1)S(1)} %pair_sum.1), channel_id=1, replica_groups=mesh['xl'=2,'zh'=4,'zl'=4,'xh'=2,'y'=4,'core'=2] {'zh'}, dimensions={0} | all-to-all | bytes 327680 | tf_op jit(solution)/shard_map/all_to_all | solution.py:283
  136.6 0.7 last_sum.1
  137.3 11.7 %all_to_all.23 = f32[8,16,256]{2,1,0:T(8,128)S(1)} all-to-all(f32[8,16,256]{2,1,0:T(8,128)S(1)} %get-tuple-element.30), channel_id=1, replica_groups=mesh['xl'=2,'zh'=4,'zl'=4,'xh'=2,'y'=4,'core'=2] {'xh','y'}, dimensions={0} | all-to-all | bytes 262144 | tf_op jit(solution)/shard_map/all_to_all | solution.py:292
  149.0 0.7 copy.14
  (3 shorter events, 0.1 us)
Async XLA Ops:
  39.4 11.1 %collective-permute-start = (bf16[16,128,128]{2,1,0:T(8,128)(2,1)S(1)}, bf16[16,128,128]{2,1,0:T(8,128)(2,1)S(1)}, u32[]{:S(2)}, u32[]{:S(2)}) collective-permute-start(bf16[16,128,128]{2,1,0:T(8,128)(2,1)S(1)} %bitcast.41), channel_id=1, source_target_pairs={{0,256},{256,0},{1,257},{257,1},{2,258},{258,2},{3,259},{259,3},{4... | collective-permute-start | bytes 1572872 | tf_op jit(solution)/shard_map/ppermute | solution.py:206
  43.5 2.2 %copy-start = (bf16[1,1,128,128,128]{4,3,2,1,0:T(8,128)(2,1)S(1)}, bf16[1,1,128,128,128]{4,3,2,1,0:T(8,128)(2,1)}, u32[]{:S(2)}) copy-start(bf16[1,1,128,128,128]{4,3,2,1,0:T(8,128)(2,1)} %param.14) | copy-start | bytes 12582916
  45.7 0.7 copy-start.6
  45.7 4.8 %copy-start.3 = (s32[1,1,128]{2,1,0:T(1,128)S(1)}, s32[1,1,128]{2,1,0:T(1,128)}, u32[]{:S(2)}) copy-start(s32[1,1,128]{2,1,0:T(1,128)} %param.15) | copy-start | bytes 1540
  46.3 24.6 %copy-start.1 = (bf16[128,256]{1,0:T(8,128)(2,1)S(1)}, bf16[128,256]{1,0:T(8,128)(2,1)}, u32[]{:S(2)}) copy-start(bf16[128,256]{1,0:T(8,128)(2,1)} %weight.1) | copy-start | bytes 196612
  46.3 24.6 %copy-start.2 = (bf16[128,256]{1,0:T(8,128)(2,1)S(1)}, bf16[128,256]{1,0:T(8,128)(2,1)}, u32[]{:S(2)}) copy-start(bf16[128,256]{1,0:T(8,128)(2,1)} %grad_out.1) | copy-start | bytes 196612
  46.3 24.6 %copy-start.4 = (f32[256]{0:T(256)S(1)}, f32[256]{0:T(256)}, u32[]{:S(2)}) copy-start(f32[256]{0:T(256)} %param.12) | copy-start | bytes 3076
  46.3 24.6 %copy-start.5 = (f32[128]{0:T(128)S(1)}, f32[128]{0:T(128)}, u32[]{:S(2)}) copy-start(f32[128]{0:T(128)} %param.11) | copy-start | bytes 1540
  53.0 3.4 %collective-permute-start.1 = (bf16[8,128,128]{2,1,0:T(8,128)(2,1)S(1)}, bf16[8,128,128]{2,1,0:T(8,128)(2,1)S(1)}, u32[]{:S(2)}, u32[]{:S(2)}) collective-permute-start(bf16[8,128,128]{2,1,0:T(8,128)(2,1)S(1)} %get-tuple-element.19), channel_id=1, source_target_pairs={{0,1},{1,0},{2,3},{3,2},{4,5},{5,4},{6,7},{7,6},{8,9},{9,8},{10,11... | collective-permute-start | bytes 786440 | tf_op jit(solution)/shard_map/ppermute | solution.py:232
  88.8 18.8 %collective-permute-start.2 = (bf16[1056,128]{1,0:T(8,128)(2,1)S(1)}, bf16[1056,128]{1,0:T(8,128)(2,1)S(1)}, u32[]{:S(2)}, u32[]{:S(2)}) collective-permute-start(bf16[1056,128]{1,0:T(8,128)(2,1)S(1)} %get-tuple-element.23), channel_id=1, source_target_pairs={{0,16},{16,32},{32,48},{48,64},{64,80},{80,96},{96,112},{112,128},... | collective-permute-start | bytes 811016 | tf_op jit(solution)/shard_map/ppermute | solution.py:198
  90.7 16.9 %collective-permute-start.3 = (bf16[1056,128]{1,0:T(8,128)(2,1)S(1)}, bf16[1056,128]{1,0:T(8,128)(2,1)S(1)}, u32[]{:S(2)}, u32[]{:S(2)}) collective-permute-start(bf16[1056,128]{1,0:T(8,128)(2,1)S(1)} %get-tuple-element.24), channel_id=1, source_target_pairs={{0,240},{16,0},{32,16},{48,32},{64,48},{80,64},{96,80},{112,96},{1... | collective-permute-start | bytes 811016 | tf_op jit(solution)/shard_map/ppermute | solution.py:198
  95.9 11.8 %collective-permute-start.4 = (bf16[544,128]{1,0:T(8,128)(2,1)S(1)}, bf16[544,128]{1,0:T(8,128)(2,1)S(1)}, u32[]{:S(2)}, u32[]{:S(2)}) collective-permute-start(bf16[544,128]{1,0:T(8,128)(2,1)S(1)} %get-tuple-element.25), channel_id=1, source_target_pairs={{0,32},{16,48},{32,64},{48,80},{64,96},{80,112},{96,128},{112,144}... | collective-permute-start | bytes 417800 | tf_op jit(solution)/shard_map/ppermute | solution.py:198
  97.8 9.8 %collective-permute-start.5 = (bf16[512,128]{1,0:T(8,128)(2,1)S(1)}, bf16[512,128]{1,0:T(8,128)(2,1)S(1)}, u32[]{:S(2)}, u32[]{:S(2)}) collective-permute-start(bf16[512,128]{1,0:T(8,128)(2,1)S(1)} %get-tuple-element.26), channel_id=1, source_target_pairs={{0,224},{16,240},{32,0},{48,16},{64,32},{80,48},{96,64},{112,80},{... | collective-permute-start | bytes 393224 | tf_op jit(solution)/shard_map/ppermute | solution.py:198
  107.8 6.9 %collective-permute-start.6 = (bf16[544,128]{1,0:T(8,128)(2,1)S(1)}, bf16[544,128]{1,0:T(8,128)(2,1)S(1)}, u32[]{:S(2)}, u32[]{:S(2)}) collective-permute-start(bf16[544,128]{1,0:T(8,128)(2,1)S(1)} %get-tuple-element.28), channel_id=1, source_target_pairs={{0,256},{256,0},{1,257},{257,1},{2,258},{258,2},{3,259},{259,3},{4... | collective-permute-start | bytes 417800 | tf_op jit(solution)/shard_map/ppermute | solution.py:274

commit v4 on v3

--- a/solution.py
+++ b/solution.py
@@ -12,6 +12,7 @@
 ROW = ("xl",) + Z
 CHIP = ("xh", "y")
 COL = CHIP + ("core",)
+FAR = ("xl", "zh")
 AXES = ROW + COL
 SIZES = (2, 4, 4, 2, 4, 2)
 
@@ -32,7 +33,6 @@
 SMEM = pl.BlockSpec(memory_space=pltpu.SMEM)
 PARAMS = pltpu.CompilerParams(vmem_limit_bytes=16 * 1024 * 1024)
 CLASS = 8
-HALF = CLASS // 2
 
 
 def split(x):
@@ -116,7 +116,7 @@
         pack[k, pl.ds(E + 16, 16)] = share[:, E:].astype(BF16)
 
 
-def backward_kernel(count, rows, places, tiles, packed, keep, up, down, up2, down2, total):
+def backward_kernel(count, rows, places, tiles, packed, keep, up, down, across, total):
     total[...] = jnp.zeros_like(total)
 
     sweep(
@@ -131,52 +131,27 @@
     for k in range(1, NC):
         grad = grad + packed[k, pl.ds(E, GW)].astype(F32)
     sent = grad.astype(BF16)
-    for ref, first, size, tail in (
-        (keep, 0, CLASS, True),
-        (up, CLASS, CLASS, True),
-        (up2, 2 * CLASS, HALF, True),
-        (down2, 2 * CLASS + HALF, HALF, False),
-        (down, 3 * CLASS, CLASS, True),
-    ):
-        for k in range(size):
-            ref[pl.ds(k * E, E)] = total[first + k].astype(BF16)
-        if tail:
-            ref[pl.ds(size * E, GW)] = sent
-
-
-def class_kernel(keep, up, down, up2, down2, mine, other):
+    for b, ref in enumerate((keep, up, across, down)):
+        for k in range(CLASS):
+            ref[pl.ds(k * E, E)] = total[b * CLASS + k].astype(BF16)
+        ref[pl.ds(CLASS * E, GW)] = sent
+
+
+def class_kernel(keep, up, down, across, pack):
+    def value(rows):
+        near = keep[rows].astype(F32) + across[rows].astype(F32)
+        return (near + (up[rows].astype(F32) + down[rows].astype(F32))).astype(BF16)
+
+    share = value(pl.ds(CLASS * E, GW))
     for k in range(CLASS):
-        rows = pl.ds(k * E, E)
-        value = keep[rows].astype(F32) + up[rows].astype(F32) + down[rows].astype(F32)
-        if k < HALF:
-            value = value + up2[rows].astype(F32)
-        else:
-            value = value + down2[pl.ds((k - HALF) * E, E)].astype(F32)
-        target = pl.ds(k // 2 * E, E)
-        if k % 2 == 0:
-            mine[target] = value
-        else:
-            other[target] = value.astype(BF16)
-    tail = pl.ds(CLASS * E, GW)
-    grad = keep[tail].astype(F32) + up[tail].astype(F32) + down[tail].astype(F32)
-    grad = grad + up2[pl.ds(HALF * E, GW)].astype(F32)
-    mine[pl.ds(HALF * E, GW)] = grad
-    other[pl.ds(HALF * E, GW)] = grad.astype(BF16)
-
-
-def pair_kernel(mine, came, pack):
-    tail = pl.ds(HALF * E, GW)
-    grad = (mine[tail] + came[tail].astype(F32)).astype(BF16)
-    for h in range(4):
-        rows = pl.ds(h * E, E)
-        pack[h, pl.ds(0, E)] = (mine[rows] + came[rows].astype(F32)).astype(BF16)
-        pack[h, pl.ds(E, GW)] = grad
+        pack[k, pl.ds(0, E)] = value(pl.ds(k * E, E))
+        pack[k, pl.ds(E, GW)] = share
 
 
 def last_kernel(terms, grad_features, pieces):
     value = terms[0].astype(F32)
-    for h in range(1, 4):
-        value = value + terms[h].astype(F32)
+    for k in range(1, CLASS):
+        value = value + terms[k].astype(F32)
     grad_features[...] = value[:E].T.astype(BF16)
     share = jnp.concatenate([value[E : E + 16], value[E + 16 :]], axis=1)
     for k in range(NCHIP):
@@ -194,12 +169,15 @@
     core = lax.axis_index("core").astype(jnp.int32).reshape(1)
     swap = [(0, 1), (1, 0)]
 
-    def up_z(x, step):
-        return lax.ppermute(x, Z, [(k, (k + step) % NZ) for k in range(NZ)])
+    def move_z(x, step):
+        return lax.ppermute(x, Z, [(k, (k + step(k)) % NZ) for k in range(NZ)])
+
+    def move_across(x):
+        return move_z(x, lambda k: 2 if k % 2 == 0 else -2)
 
     flipped = jnp.bitwise_xor(cols // NZ, lax.axis_index("xl"))
     residue = jnp.mod(cols - lax.axis_index("zl"), 4)
-    places = (residue * CLASS + (cols // 4) % 4 * 2 + flipped).astype(jnp.int32)
+    places = (residue * CLASS + cols // NZ * 4 + cols // 4 % 4).astype(jnp.int32)
     sources = (flipped * NZ + cols % NZ).astype(jnp.int32)
 
     near = lax.all_gather(features, Z, axis=0, tiled=True).reshape(NZ, E, E)
@@ -250,37 +228,26 @@
     packed = lax.all_to_all(pack, CHIP, 0, 0, tiled=True)
     packed = lax.all_gather(packed, "core", axis=0, tiled=True)
 
-    def line(blocks, tail=GW):
-        return shape((blocks * E + tail, E))
-
-    keep, up, down, up2, down2 = pl.pallas_call(
+    line = shape((CLASS * E + GW, E))
+    keep, up, down, across = pl.pallas_call(
         backward_kernel,
-        out_shape=(line(CLASS), line(CLASS), line(CLASS), line(HALF), line(HALF, 0)),
+        out_shape=(line,) * 4,
         in_specs=[SMEM] * 3 + [VMEM] * 2,
-        out_specs=(VMEM,) * 5,
+        out_specs=(VMEM,) * 4,
         scratch_shapes=[pltpu.VMEM((NR + 1, E, E), F32)],
         compiler_params=PARAMS,
         name="backward_sweep",
     )(count, rows, places, tiles, packed)
-    arrived = [up_z(up, 1), up_z(down, -1), up_z(up2, 2), up_z(down2, -2)]
-    mine, other = pl.pallas_call(
+    arrived = [move_z(up, lambda k: 1), move_z(down, lambda k: -1), move_across(across)]
+    classes = pl.pallas_call(
         class_kernel,
-        out_shape=(shape((HALF * E + GW, E), F32), line(HALF)),
-        in_specs=[VMEM] * 5,
-        out_specs=(VMEM, VMEM),
+        out_shape=shape((CLASS, PACK, E)),
+        in_specs=[VMEM] * 4,
+        out_specs=VMEM,
         compiler_params=PARAMS,
         name="class_sum",
     )(keep, *arrived)
-    came = lax.ppermute(other, "xl", swap)
-    pairs = pl.pallas_call(
-        pair_kernel,
-        out_shape=shape((4, E + GW, E)),
-        in_specs=[VMEM] * 2,
-        out_specs=VMEM,
-        compiler_params=PARAMS,
-        name="pair_sum",
-    )(mine, came)
-    column = lax.all_to_all(pairs, "zh", 0, 0, tiled=True)
+    column = lax.all_to_all(classes, FAR, 0, 0, tiled=True)
     grad_features, pieces = pl.pallas_call(
         last_kernel,
         out_shape=(shape((E, E)), shape((NCHIP, 16, WIDE), F32)),

time: 150 us -> 149 us (level)
  the two profiles are of different devices: /device:TPU:8 before, /device:TPU:1 now
where the time goes in v4:
time: 149 us; the launch traced here: 147 us
  blocking collectives  100 us (67%)
  starting transfers between devices  22.8 us (15%)
  waiting for transfers between devices  13.5 us (9%)
  Pallas kernels  5.48 us (4%)
  local copies, waits for them, and re-layouts  3.14 us (2%)
    all_gather x1, blocking collectives, on_device(): near = lax.all_gather(features, Z, axis=0, tiled=True).reshape(NZ, E, E)  32.1 us
    all_to_all x1, blocking collectives, on_device(): column = lax.all_to_all(classes, FAR, 0, 0, tiled=True)  29 us
    all_to_all x1, blocking collectives, on_device(): terms = lax.all_to_all(partial, CHIP, 0, 0, tiled=True)  14 us
    all_to_all x1, blocking collectives, on_device(): packed = lax.all_to_all(pack, CHIP, 0, 0, tiled=True)  11.4 us
    ppermute x1, starting transfers between devices, on_device(): came = lax.ppermute(far, 'core', swap)  11.3 us
    all_to_all x1, blocking collectives, on_device(): lax.all_to_all(pieces, CHIP, 0, 0, tiled=True).reshape(E, WIDE)  9.34 us
    ppermute x3, waiting for transfers between devices, move_z(): return lax.ppermute(x, Z, [(k, (k + step(k)) % NZ) for k in range(NZ)])  9.12 us
    ppermute x3, starting transfers between devices, move_z(): return lax.ppermute(x, Z, [(k, (k + step(k)) % NZ) for k in range(NZ)])  8.41 us
  transfers between devices with their start and end apart: 5, of which 5 were waited for; matrix products, arithmetic and copies ran while one was open for 0% of the time, Pallas kernels for 0%

profile of v4, /device:TPU:1, one launch (start us, length us, event | category | flops | bytes accessed | tf_op | source)
XLA Modules:
  0.0 146.6 jit_solution(11523900238888128977)
XLA Ops:
  0.6 32.1 %all_gather.6 = bf16[2048,128]{1,0:T(8,128)(2,1)S(1)} all-gather(bf16[128,128]{1,0:T(8,128)(2,1)} %param.9), channel_id=1, replica_groups=mesh['xl'=2,'zh'=4,'zl'=4,'xh'=2,'y'=4,'core'=2] {'zh','zl'}, dimensions={0}, use_global_device_ids=true | all-gather | bytes 557056 | tf_op jit(solution)/shard_map/all_gather | solution.py:183
  32.7 3.1 %collective-permute-start = (bf16[16,128,128]{2,1,0:T(8,128)(2,1)S(1)}, bf16[16,128,128]{2,1,0:T(8,128)(2,1)S(1)}, u32[]{:S(2)}, u32[]{:S(2)}) collective-permute-start(bf16[16,128,128]{2,1,0:T(8,128)(2,1)S(1)} %bitcast.41), channel_id=1, source_target_pairs={{0,256},{256,0},{1,257},{257,1},{2,258},{258,2},{3,259},{259,3},{4... | collective-permute-start | bytes 1572872 | tf_op jit(solution)/shard_map/ppermute | solution.py:184
  36.5 0.0 copy-start
  36.5 2.2 %copy-done = bf16[1,1,128,128,128]{4,3,2,1,0:T(8,128)(2,1)S(1)} copy-done((bf16[1,1,128,128,128]{4,3,2,1,0:T(8,128)(2,1)S(1)}, bf16[1,1,128,128,128]{4,3,2,1,0:T(8,128)(2,1)}, u32[]{:S(2)}) %copy-start) | copy-done | bytes 4194328
  38.7 0.0 copy-start.6
  38.7 0.0 copy-start.3
  38.7 0.4 preload.1.tiles
  39.0 0.3 copy-done.6
  39.3 0.0 copy-start.1
  39.3 0.0 copy-start.2
  39.3 0.0 copy-start.4
  39.3 0.0 copy-start.5
  39.4 3.2 %collective-permute-done.peer = bf16[16,128,128]{2,1,0:T(8,128)(2,1)S(1)} collective-permute-done((bf16[16,128,128]{2,1,0:T(8,128)(2,1)S(1)}, bf16[16,128,128]{2,1,0:T(8,128)(2,1)S(1)}, u32[]{:S(2)}, u32[]{:S(2)}) %collective-permute-start) | collective-permute-done | bytes 524320 | tf_op jit(solution)/shard_map/ppermute | solution.py:184
  42.6 0.0 copy-done.3
  42.6 1.6 %forward_sweep.1 = (bf16[8,128,128]{2,1,0:T(8,128)(2,1)S(1)}, bf16[8,128,128]{2,1,0:T(8,128)(2,1)S(1)}) custom-call(s32[1]{0:T(128)} %bitcast.38.count, s32[128]{0:T(128)S(1)} %bitcast.43, s32[128]{0:T(128)S(1)} %fusion.places, s32[1]{0:T(128)} %bitcast.3.core, bf16[128,128,128]{2,1,0:T(8,128)(2,1)S(1)} %preload.1.tiles, bf16[16,128,128]{2,1,0:T(8,128)(2,1)S(1)} %bitcast.42, ...), custom_call_target="tpu_custom_call" | custom-call | tf_op jit(solution)/shard_map/forward_sweep/pallas_call | solution.py:197
  44.3 11.3 %collective-permute-start.1 = (bf16[8,128,128]{2,1,0:T(8,128)(2,1)S(1)}, bf16[8,128,128]{2,1,0:T(8,128)(2,1)S(1)}, u32[]{:S(2)}, u32[]{:S(2)}) collective-permute-start(bf16[8,128,128]{2,1,0:T(8,128)(2,1)S(1)} %get-tuple-element.16), channel_id=1, source_target_pairs={{0,1},{1,0},{2,3},{3,2},{4,5},{5,4},{6,7},{7,6},{8,9},{9,8},{10,11... | collective-permute-start | bytes 786440 | tf_op jit(solution)/shard_map/ppermute | solution.py:210
  55.6 1.1 collective-permute-done.1.far
  56.7 0.1 chip_sum.1
  56.8 14.0 %all_to_all.20.terms = bf16[8,128,128]{2,1,0:T(8,128)(2,1)S(1)} all-to-all(bf16[8,128,128]{2,1,0:T(8,128)(2,1)S(1)} %chip_sum.1), channel_id=1, replica_groups=mesh['xl'=2,'zh'=4,'zl'=4,'xh'=2,'y'=4,'core'=2] {'xh','y'}, dimensions={0} | all-to-all | bytes 524288 | tf_op jit(solution)/shard_map/all_to_all | solution.py:219
  70.8 0.0 copy-done.1
  70.8 0.0 copy-done.2
  70.8 0.0 copy-done.4
  70.8 0.0 copy-done.5
  70.8 0.9 node_update.1
  71.7 11.4 %all_to_all.21 = bf16[8,160,128]{2,1,0:T(8,128)(2,1)S(1)} all-to-all(bf16[8,160,128]{2,1,0:T(8,128)(2,1)S(1)} %get-tuple-element.18), channel_id=1, replica_groups=mesh['xl'=2,'zh'=4,'zl'=4,'xh'=2,'y'=4,'core'=2] {'xh','y'}, dimensions={0} | all-to-all | bytes 655360 | tf_op jit(solution)/shard_map/all_to_all | solution.py:228
  83.1 4.4 %all_gather.7.packed = bf16[16,160,128]{2,1,0:T(8,128)(2,1)S(1)} all-gather(bf16[8,160,128]{2,1,0:T(8,128)(2,1)S(1)} %all_to_all.21), channel_id=1, replica_groups=mesh['xl'=2,'zh'=4,'zl'=4,'xh'=2,'y'=4,'core'=2] {'core'}, dimensions={0}, use_global_device_ids=true | all-gather | bytes 983040 | tf_op jit(solution)/shard_map/all_gather | solution.py:229
  87.5 1.7 %backward_sweep.1 = (bf16[1056,128]{1,0:T(8,128)(2,1)S(1)}, bf16[1056,128]{1,0:T(8,128)(2,1)S(1)}, bf16[1056,128]{1,0:T(8,128)(2,1)S(1)}, bf16[1056,128]{1,0:T(8,128)(2,1)S(1)}) custom-call(s32[1]{0:T(128)} %bitcast.39.count, s32[128]{0:T(128)S(1)} %bitcast.44, s32[128]{0:T(128)S(1)} %get-tuple-element.25.places, bf16[128,128,128]{2,1,0:T(8,128)(2,1)S(1)} %preload.1.tiles, ...), custom_call_target="tpu_custom_call" | custom-call | tf_op jit(solution)/shard_map/backward_sweep/pallas_call | solution.py:232
  89.2 1.9 %collective-permute-start.2 = (bf16[1056,128]{1,0:T(8,128)(2,1)S(1)}, bf16[1056,128]{1,0:T(8,128)(2,1)S(1)}, u32[]{:S(2)}, u32[]{:S(2)}) collective-permute-start(bf16[1056,128]{1,0:T(8,128)(2,1)S(1)} %get-tuple-element.20), channel_id=1, source_target_pairs={{0,16},{16,32},{32,48},{48,64},{64,80},{80,96},{96,112},{112,128},... | collective-permute-start | bytes 811016 | tf_op jit(solution)/shard_map/ppermute | solution.py:173
  91.1 4.6 %collective-permute-start.3 = (bf16[1056,128]{1,0:T(8,128)(2,1)S(1)}, bf16[1056,128]{1,0:T(8,128)(2,1)S(1)}, u32[]{:S(2)}, u32[]{:S(2)}) collective-permute-start(bf16[1056,128]{1,0:T(8,128)(2,1)S(1)} %get-tuple-element.21), channel_id=1, source_target_pairs={{0,240},{16,0},{32,16},{48,32},{64,48},{80,64},{96,80},{112,96},{1... | collective-permute-start | bytes 811016 | tf_op jit(solution)/shard_map/ppermute | solution.py:173
  95.7 1.9 %collective-permute-start.4 = (bf16[1056,128]{1,0:T(8,128)(2,1)S(1)}, bf16[1056,128]{1,0:T(8,128)(2,1)S(1)}, u32[]{:S(2)}, u32[]{:S(2)}) collective-permute-start(bf16[1056,128]{1,0:T(8,128)(2,1)S(1)} %get-tuple-element.22), channel_id=1, source_target_pairs={{0,32},{16,240},{32,64},{48,16},{64,96},{80,48},{96,128},{112,80},... | collective-permute-start | bytes 811016 | tf_op jit(solution)/shard_map/ppermute | solution.py:173
  97.6 2.4 %collective-permute-done.2.up = bf16[1056,128]{1,0:T(8,128)(2,1)S(1)} collective-permute-done((bf16[1056,128]{1,0:T(8,128)(2,1)S(1)}, bf16[1056,128]{1,0:T(8,128)(2,1)S(1)}, u32[]{:S(2)}, u32[]{:S(2)}) %collective-permute-start.2) | collective-permute-done | bytes 270368 | tf_op jit(solution)/shard_map/ppermute | solution.py:173
  100.0 1.5 %collective-permute-done.3.down = bf16[1056,128]{1,0:T(8,128)(2,1)S(1)} collective-permute-done((bf16[1056,128]{1,0:T(8,128)(2,1)S(1)}, bf16[1056,128]{1,0:T(8,128)(2,1)S(1)}, u32[]{:S(2)}, u32[]{:S(2)}) %collective-permute-start.3) | collective-permute-done | bytes 270368 | tf_op jit(solution)/shard_map/ppermute | solution.py:173
  101.5 5.2 %collective-permute-done.4.across = bf16[1056,128]{1,0:T(8,128)(2,1)S(1)} collective-permute-done((bf16[1056,128]{1,0:T(8,128)(2,1)S(1)}, bf16[1056,128]{1,0:T(8,128)(2,1)S(1)}, u32[]{:S(2)}, u32[]{:S(2)}) %collective-permute-start.4) | collective-permute-done | bytes 270368 | tf_op jit(solution)/shard_map/ppermute | solution.py:173
  106.8 0.1 class_sum.1
  106.9 29.0 %all_to_all.22.terms = bf16[8,160,128]{2,1,0:T(8,128)(2,1)S(1)} all-to-all(bf16[8,160,128]{2,1,0:T(8,128)(2,1)S(1)} %class_sum.1), channel_id=1, replica_groups=mesh['xl'=2,'zh'=4,'zl'=4,'xh'=2,'y'=4,'core'=2] {'xl','zh'}, dimensions={0} | all-to-all | bytes 655360 | tf_op jit(solution)/shard_map/all_to_all | solution.py:250
  135.9 0.7 last_sum.1
  136.6 9.3 %all_to_all.23 = f32[8,16,256]{2,1,0:T(8,128)S(1)} all-to-all(f32[8,16,256]{2,1,0:T(8,128)S(1)} %get-tuple-element.24), channel_id=1, replica_groups=mesh['xl'=2,'zh'=4,'zl'=4,'xh'=2,'y'=4,'core'=2] {'xh','y'}, dimensions={0} | all-to-all | bytes 262144 | tf_op jit(solution)/shard_map/all_to_all | solution.py:259
  145.9 0.7 copy.14
  (2 shorter events, 0.0 us)
Async XLA Ops:
  32.7 9.9 %collective-permute-start = (bf16[16,128,128]{2,1,0:T(8,128)(2,1)S(1)}, bf16[16,128,128]{2,1,0:T(8,128)(2,1)S(1)}, u32[]{:S(2)}, u32[]{:S(2)}) collective-permute-start(bf16[16,128,128]{2,1,0:T(8,128)(2,1)S(1)} %bitcast.41), channel_id=1, source_target_pairs={{0,256},{256,0},{1,257},{257,1},{2,258},{258,2},{3,259},{259,3},{4... | collective-permute-start | bytes 1572872 | tf_op jit(solution)/shard_map/ppermute | solution.py:184
  36.5 2.2 %copy-start = (bf16[1,1,128,128,128]{4,3,2,1,0:T(8,128)(2,1)S(1)}, bf16[1,1,128,128,128]{4,3,2,1,0:T(8,128)(2,1)}, u32[]{:S(2)}) copy-start(bf16[1,1,128,128,128]{4,3,2,1,0:T(8,128)(2,1)} %param.14) | copy-start | bytes 12582916
  38.7 0.7 copy-start.6
  38.7 4.0 %copy-start.3 = (s32[1,1,128]{2,1,0:T(1,128)S(1)}, s32[1,1,128]{2,1,0:T(1,128)}, u32[]{:S(2)}) copy-start(s32[1,1,128]{2,1,0:T(1,128)} %param.15) | copy-start | bytes 1540
  39.3 31.5 %copy-start.1 = (bf16[128,256]{1,0:T(8,128)(2,1)S(1)}, bf16[128,256]{1,0:T(8,128)(2,1)}, u32[]{:S(2)}) copy-start(bf16[128,256]{1,0:T(8,128)(2,1)} %weight.1) | copy-start | bytes 196612
  39.3 31.5 %copy-start.2 = (bf16[128,256]{1,0:T(8,128)(2,1)S(1)}, bf16[128,256]{1,0:T(8,128)(2,1)}, u32[]{:S(2)}) copy-start(bf16[128,256]{1,0:T(8,128)(2,1)} %grad_out.1) | copy-start | bytes 196612
  39.3 31.5 %copy-start.4 = (f32[256]{0:T(256)S(1)}, f32[256]{0:T(256)}, u32[]{:S(2)}) copy-start(f32[256]{0:T(256)} %param.12) | copy-start | bytes 3076
  39.3 31.5 %copy-start.5 = (f32[128]{0:T(128)S(1)}, f32[128]{0:T(128)}, u32[]{:S(2)}) copy-start(f32[128]{0:T(128)} %param.11) | copy-start | bytes 1540
  44.3 12.5 %collective-permute-start.1 = (bf16[8,128,128]{2,1,0:T(8,128)(2,1)S(1)}, bf16[8,128,128]{2,1,0:T(8,128)(2,1)S(1)}, u32[]{:S(2)}, u32[]{:S(2)}) collective-permute-start(bf16[8,128,128]{2,1,0:T(8,128)(2,1)S(1)} %get-tuple-element.16), channel_id=1, source_target_pairs={{0,1},{1,0},{2,3},{3,2},{4,5},{5,4},{6,7},{7,6},{8,9},{9,8},{10,11... | collective-permute-start | bytes 786440 | tf_op jit(solution)/shard_map/ppermute | solution.py:210
  89.2 10.8 %collective-permute-start.2 = (bf16[1056,128]{1,0:T(8,128)(2,1)S(1)}, bf16[1056,128]{1,0:T(8,128)(2,1)S(1)}, u32[]{:S(2)}, u32[]{:S(2)}) collective-permute-start(bf16[1056,128]{1,0:T(8,128)(2,1)S(1)} %get-tuple-element.20), channel_id=1, source_target_pairs={{0,16},{16,32},{32,48},{48,64},{64,80},{80,96},{96,112},{112,128},... | collective-permute-start | bytes 811016 | tf_op jit(solution)/shard_map/ppermute | solution.py:173
  91.1 10.4 %collective-permute-start.3 = (bf16[1056,128]{1,0:T(8,128)(2,1)S(1)}, bf16[1056,128]{1,0:T(8,128)(2,1)S(1)}, u32[]{:S(2)}, u32[]{:S(2)}) collective-permute-start(bf16[1056,128]{1,0:T(8,128)(2,1)S(1)} %get-tuple-element.21), channel_id=1, source_target_pairs={{0,240},{16,0},{32,16},{48,32},{64,48},{80,64},{96,80},{112,96},{1... | collective-permute-start | bytes 811016 | tf_op jit(solution)/shard_map/ppermute | solution.py:173
  95.7 11.1 %collective-permute-start.4 = (bf16[1056,128]{1,0:T(8,128)(2,1)S(1)}, bf16[1056,128]{1,0:T(8,128)(2,1)S(1)}, u32[]{:S(2)}, u32[]{:S(2)}) collective-permute-start(bf16[1056,128]{1,0:T(8,128)(2,1)S(1)} %get-tuple-element.22), channel_id=1, source_target_pairs={{0,32},{16,240},{32,64},{48,16},{64,96},{80,48},{96,128},{112,80},... | collective-permute-start | bytes 811016 | tf_op jit(solution)/shard_map/ppermute | solution.py:173

commit v5 on v4

--- a/solution.py
+++ b/solution.py
@@ -8,13 +8,14 @@
 
 F32 = jnp.float32
 BF16 = jnp.bfloat16
-Z = ("zh", "zl")
+Z = ("zh", "z1", "z0")
 ROW = ("xl",) + Z
 CHIP = ("xh", "y")
 COL = CHIP + ("core",)
-FAR = ("xl", "zh")
+QUAD = ("xl", "z0")
+FAR = ("zh", "z1")
 AXES = ROW + COL
-SIZES = (2, 4, 4, 2, 4, 2)
+SIZES = (2, 4, 2, 2, 2, 4, 2)
 
 E = 128
 WIDE = 256
@@ -25,6 +26,8 @@
 NR = NX * NZ
 GW = 32
 PACK = E + GW
+CLASS = 8
+LINE = CLASS * E + GW
 UNROLL = 64
 NCHIP = 8
 
@@ -32,7 +35,6 @@
 VMEM = pl.BlockSpec(memory_space=pltpu.VMEM)
 SMEM = pl.BlockSpec(memory_space=pltpu.SMEM)
 PARAMS = pltpu.CompilerParams(vmem_limit_bytes=16 * 1024 * 1024)
-CLASS = 8
 
 
 def split(x):
@@ -116,7 +118,7 @@
         pack[k, pl.ds(E + 16, 16)] = share[:, E:].astype(BF16)
 
 
-def backward_kernel(count, rows, places, tiles, packed, keep, up, down, across, total):
+def backward_kernel(count, rows, places, tiles, packed, parts, total):
     total[...] = jnp.zeros_like(total)
 
     sweep(
@@ -131,16 +133,16 @@
     for k in range(1, NC):
         grad = grad + packed[k, pl.ds(E, GW)].astype(F32)
     sent = grad.astype(BF16)
-    for b, ref in enumerate((keep, up, across, down)):
+    for b in range(4):
         for k in range(CLASS):
-            ref[pl.ds(k * E, E)] = total[b * CLASS + k].astype(BF16)
-        ref[pl.ds(CLASS * E, GW)] = sent
-
-
-def class_kernel(keep, up, down, across, pack):
+            parts[b, pl.ds(k * E, E)] = total[b * CLASS + k].astype(BF16)
+        parts[b, pl.ds(CLASS * E, GW)] = sent
+
+
+def class_kernel(parts, pack):
     def value(rows):
-        near = keep[rows].astype(F32) + across[rows].astype(F32)
-        return (near + (up[rows].astype(F32) + down[rows].astype(F32))).astype(BF16)
+        first = parts[0, rows].astype(F32) + parts[1, rows].astype(F32)
+        return (first + (parts[2, rows].astype(F32) + parts[3, rows].astype(F32))).astype(BF16)
 
     share = value(pl.ds(CLASS * E, GW))
     for k in range(CLASS):
@@ -169,15 +171,8 @@
     core = lax.axis_index("core").astype(jnp.int32).reshape(1)
     swap = [(0, 1), (1, 0)]
 
-    def move_z(x, step):
-        return lax.ppermute(x, Z, [(k, (k + step(k)) % NZ) for k in range(NZ)])
-
-    def move_across(x):
-        return move_z(x, lambda k: 2 if k % 2 == 0 else -2)
-
     flipped = jnp.bitwise_xor(cols // NZ, lax.axis_index("xl"))
-    residue = jnp.mod(cols - lax.axis_index("zl"), 4)
-    places = (residue * CLASS + cols // NZ * 4 + cols // 4 % 4).astype(jnp.int32)
+    places = ((cols // NZ * 2 + cols % 2) * CLASS + cols // 2 % CLASS).astype(jnp.int32)
     sources = (flipped * NZ + cols % NZ).astype(jnp.int32)
 
     near = lax.all_gather(features, Z, axis=0, tiled=True).reshape(NZ, E, E)
@@ -228,25 +223,24 @@
     packed = lax.all_to_all(pack, CHIP, 0, 0, tiled=True)
     packed = lax.all_gather(packed, "core", axis=0, tiled=True)
 
-    line = shape((CLASS * E + GW, E))
-    keep, up, down, across = pl.pallas_call(
+    parts = pl.pallas_call(
         backward_kernel,
-        out_shape=(line,) * 4,
+        out_shape=shape((4, LINE, E)),
         in_specs=[SMEM] * 3 + [VMEM] * 2,
-        out_specs=(VMEM,) * 4,
+        out_specs=VMEM,
         scratch_shapes=[pltpu.VMEM((NR + 1, E, E), F32)],
         compiler_params=PARAMS,
         name="backward_sweep",
     )(count, rows, places, tiles, packed)
-    arrived = [move_z(up, lambda k: 1), move_z(down, lambda k: -1), move_across(across)]
+    parts = lax.all_to_all(parts, QUAD, 0, 0, tiled=True)
     classes = pl.pallas_call(
         class_kernel,
         out_shape=shape((CLASS, PACK, E)),
-        in_specs=[VMEM] * 4,
+        in_specs=[VMEM],
         out_specs=VMEM,
         compiler_params=PARAMS,
         name="class_sum",
-    )(keep, *arrived)
+    )(parts)
     column = lax.all_to_all(classes, FAR, 0, 0, tiled=True)
     grad_features, pieces = pl.pallas_call(
         last_kernel,

time: 149 us -> 148 us (level)
  the two profiles are of different devices: /device:TPU:1 before, /device:TPU:2 now
where the time goes in v5:
time: 148 us
  blocking collectives  127 us (86%)
  waiting for transfers between devices  6.57 us (4%)
  Pallas kernels  5.49 us (4%)
  starting transfers between devices  4.35 us (3%)
  local copies, waits for them, and re-layouts  3.14 us (2%)
    all_gather x1, blocking collectives, on_device(): near = lax.all_gather(features, Z, axis=0, tiled=True).reshape(NZ, E, E)  38.8 us
    all_to_all x1, blocking collectives, on_device(): column = lax.all_to_all(classes, FAR, 0, 0, tiled=True)  30.9 us
    all_to_all x1, blocking collectives, on_device(): parts = lax.all_to_all(parts, QUAD, 0, 0, tiled=True)  17.8 us
    all_to_all x1, blocking collectives, on_device(): terms = lax.all_to_all(partial, CHIP, 0, 0, tiled=True)  14.8 us
    all_to_all x1, blocking collectives, on_device(): packed = lax.all_to_all(pack, CHIP, 0, 0, tiled=True)  11.8 us
    all_to_all x1, blocking collectives, on_device(): lax.all_to_all(pieces, CHIP, 0, 0, tiled=True).reshape(E, WIDE)  10.5 us
    ppermute x1, waiting for transfers between devices, on_device(): peer = lax.ppermute(near, 'xl', swap)  5.07 us
    unnamed x15, local copies, waits for them, and re-layouts  3.14 us
  transfers between devices with their start and end apart: 2, of which 2 were waited for; matrix products, arithmetic and copies ran while one was open for 0% of the time, Pallas kernels for 0%

profile of v5, /device:TPU:2, one launch (start us, length us, event | category | flops | bytes accessed | tf_op | source)
XLA Modules:
  0.0 147.9 jit_solution(1387636262155367253)
XLA Ops:
  0.6 38.8 %all_gather.6 = bf16[2048,128]{1,0:T(8,128)(2,1)S(1)} all-gather(bf16[128,128]{1,0:T(8,128)(2,1)} %param.9), channel_id=1, replica_groups=mesh['xl'=2,'zh'=4,'z1'=2,'z0'=2,'xh'=2,'y'=4,'core'=2] {'zh','z1','z0'}, dimensions={0}, use_global_device_ids=true | all-gather | bytes 557056 | tf_op jit(solution)/shard_map/all_gather | solution.py:178
  39.4 2.4 %collective-permute-start = (bf16[16,128,128]{2,1,0:T(8,128)(2,1)S(1)}, bf16[16,128,128]{2,1,0:T(8,128)(2,1)S(1)}, u32[]{:S(2)}, u32[]{:S(2)}) collective-permute-start(bf16[16,128,128]{2,1,0:T(8,128)(2,1)S(1)} %bitcast.38), channel_id=1, source_target_pairs={{0,256},{256,0},{1,257},{257,1},{2,258},{258,2},{3,259},{259,3},{4... | collective-permute-start | bytes 1572872 | tf_op jit(solution)/shard_map/ppermute | solution.py:179
  42.5 0.0 copy-start
  42.5 2.2 %copy-done = bf16[1,1,128,128,128]{4,3,2,1,0:T(8,128)(2,1)S(1)} copy-done((bf16[1,1,128,128,128]{4,3,2,1,0:T(8,128)(2,1)S(1)}, bf16[1,1,128,128,128]{4,3,2,1,0:T(8,128)(2,1)}, u32[]{:S(2)}) %copy-start) | copy-done | bytes 4194328
  44.7 0.0 copy-start.6
  44.7 0.0 copy-start.3
  44.7 0.4 preload.1.tiles
  45.1 0.3 copy-done.6
  45.4 0.0 copy-start.1
  45.4 0.0 copy-start.2
  45.4 0.0 copy-start.4
  45.4 0.0 copy-start.5
  45.4 5.1 %collective-permute-done.peer = bf16[16,128,128]{2,1,0:T(8,128)(2,1)S(1)} collective-permute-done((bf16[16,128,128]{2,1,0:T(8,128)(2,1)S(1)}, bf16[16,128,128]{2,1,0:T(8,128)(2,1)S(1)}, u32[]{:S(2)}, u32[]{:S(2)}) %collective-permute-start) | collective-permute-done | bytes 524320 | tf_op jit(solution)/shard_map/ppermute | solution.py:179
  50.5 0.0 copy-done.3
  50.5 1.7 %forward_sweep.1 = (bf16[8,128,128]{2,1,0:T(8,128)(2,1)S(1)}, bf16[8,128,128]{2,1,0:T(8,128)(2,1)S(1)}) custom-call(s32[1]{0:T(128)} %bitcast.35.count, s32[128]{0:T(128)S(1)} %bitcast.40, s32[128]{0:T(128)S(1)} %fusion.places, s32[1]{0:T(128)} %bitcast.3.core, bf16[128,128,128]{2,1,0:T(8,128)(2,1)S(1)} %preload.1.tiles, bf16[16,128,128]{2,1,0:T(8,128)(2,1)S(1)} %bitcast.39, ...), custom_call_target="tpu_custom_call" | custom-call | tf_op jit(solution)/shard_map/forward_sweep/pallas_call | solution.py:192
  52.2 1.9 %collective-permute-start.1 = (bf16[8,128,128]{2,1,0:T(8,128)(2,1)S(1)}, bf16[8,128,128]{2,1,0:T(8,128)(2,1)S(1)}, u32[]{:S(2)}, u32[]{:S(2)}) collective-permute-start(bf16[8,128,128]{2,1,0:T(8,128)(2,1)S(1)} %get-tuple-element.12), channel_id=1, source_target_pairs={{0,1},{1,0},{2,3},{3,2},{4,5},{5,4},{6,7},{7,6},{8,9},{9,8},{10,11... | collective-permute-start | bytes 786440 | tf_op jit(solution)/shard_map/ppermute | solution.py:205
  54.1 1.5 %collective-permute-done.1.far = bf16[8,128,128]{2,1,0:T(8,128)(2,1)S(1)} collective-permute-done((bf16[8,128,128]{2,1,0:T(8,128)(2,1)S(1)}, bf16[8,128,128]{2,1,0:T(8,128)(2,1)S(1)}, u32[]{:S(2)}, u32[]{:S(2)}) %collective-permute-start.1) | collective-permute-done | bytes 262176 | tf_op jit(solution)/shard_map/ppermute | solution.py:205
  55.6 0.1 chip_sum.1
  55.7 14.8 %all_to_all.25.terms = bf16[8,128,128]{2,1,0:T(8,128)(2,1)S(1)} all-to-all(bf16[8,128,128]{2,1,0:T(8,128)(2,1)S(1)} %chip_sum.1), channel_id=1, replica_groups=mesh['xl'=2,'zh'=4,'z1'=2,'z0'=2,'xh'=2,'y'=4,'core'=2] {'xh','y'}, dimensions={0} | all-to-all | bytes 524288 | tf_op jit(solution)/shard_map/all_to_all | solution.py:214
  70.5 0.0 copy-done.1
  70.5 0.0 copy-done.2
  70.5 0.0 copy-done.4
  70.5 0.0 copy-done.5
  70.5 0.9 node_update.1
  71.4 11.8 %all_to_all.26 = bf16[8,160,128]{2,1,0:T(8,128)(2,1)S(1)} all-to-all(bf16[8,160,128]{2,1,0:T(8,128)(2,1)S(1)} %get-tuple-element.14), channel_id=1, replica_groups=mesh['xl'=2,'zh'=4,'z1'=2,'z0'=2,'xh'=2,'y'=4,'core'=2] {'xh','y'}, dimensions={0} | all-to-all | bytes 655360 | tf_op jit(solution)/shard_map/all_to_all | solution.py:223
  83.2 2.3 %all_gather.7.packed = bf16[16,160,128]{2,1,0:T(8,128)(2,1)S(1)} all-gather(bf16[8,160,128]{2,1,0:T(8,128)(2,1)S(1)} %all_to_all.26), channel_id=1, replica_groups=mesh['xl'=2,'zh'=4,'z1'=2,'z0'=2,'xh'=2,'y'=4,'core'=2] {'core'}, dimensions={0}, use_global_device_ids=true | all-gather | bytes 983040 | tf_op jit(solution)/shard_map/all_gather | solution.py:224
  85.5 1.7 %backward_sweep.1 = bf16[4,1056,128]{2,1,0:T(8,128)(2,1)S(1)} custom-call(s32[1]{0:T(128)} %bitcast.36.count, s32[128]{0:T(128)S(1)} %bitcast.41, s32[128]{0:T(128)S(1)} %get-tuple-element.17.places, bf16[128,128,128]{2,1,0:T(8,128)(2,1)S(1)} %preload.1.tiles, bf16[16,160,128]{2,1,0:T(8,128)(2,1)S(1)} %all_gather.7.packed), custom_call_target="tpu_custom_call" | custom-call | tf_op jit(solution)/shard_map/backward_sweep/pallas_call | solution.py:226
  87.2 17.8 %all_to_all.27.parts = bf16[4,1056,128]{2,1,0:T(8,128)(2,1)S(1)} all-to-all(bf16[4,1056,128]{2,1,0:T(8,128)(2,1)S(1)} %backward_sweep.1), channel_id=1, replica_groups=mesh['xl'=2,'zh'=4,'z1'=2,'z0'=2,'xh'=2,'y'=4,'core'=2] {'xl','z0'}, dimensions={0} | all-to-all | bytes 2162688 | tf_op jit(solution)/shard_map/all_to_all | solution.py:235
  105.0 0.1 class_sum.1
  105.1 30.9 %all_to_all.28.terms = bf16[8,160,128]{2,1,0:T(8,128)(2,1)S(1)} all-to-all(bf16[8,160,128]{2,1,0:T(8,128)(2,1)S(1)} %class_sum.1), channel_id=1, replica_groups=mesh['xl'=2,'zh'=4,'z1'=2,'z0'=2,'xh'=2,'y'=4,'core'=2] {'zh','z1'}, dimensions={0} | all-to-all | bytes 655360 | tf_op jit(solution)/shard_map/all_to_all | solution.py:244
  136.0 0.7 last_sum.1
  136.8 10.5 %all_to_all.29 = f32[8,16,256]{2,1,0:T(8,128)S(1)} all-to-all(f32[8,16,256]{2,1,0:T(8,128)S(1)} %get-tuple-element.16), channel_id=1, replica_groups=mesh['xl'=2,'zh'=4,'z1'=2,'z0'=2,'xh'=2,'y'=4,'core'=2] {'xh','y'}, dimensions={0} | all-to-all | bytes 262144 | tf_op jit(solution)/shard_map/all_to_all | solution.py:253
  147.2 0.7 copy.14
  (2 shorter events, 0.0 us)
Async XLA Ops:
  39.4 11.1 %collective-permute-start = (bf16[16,128,128]{2,1,0:T(8,128)(2,1)S(1)}, bf16[16,128,128]{2,1,0:T(8,128)(2,1)S(1)}, u32[]{:S(2)}, u32[]{:S(2)}) collective-permute-start(bf16[16,128,128]{2,1,0:T(8,128)(2,1)S(1)} %bitcast.38), channel_id=1, source_target_pairs={{0,256},{256,0},{1,257},{257,1},{2,258},{258,2},{3,259},{259,3},{4... | collective-permute-start | bytes 1572872 | tf_op jit(solution)/shard_map/ppermute | solution.py:179
  42.5 2.2 %copy-start = (bf16[1,1,128,128,128]{4,3,2,1,0:T(8,128)(2,1)S(1)}, bf16[1,1,128,128,128]{4,3,2,1,0:T(8,128)(2,1)}, u32[]{:S(2)}) copy-start(bf16[1,1,128,128,128]{4,3,2,1,0:T(8,128)(2,1)} %param.14) | copy-start | bytes 12582916
  44.7 0.7 copy-start.6
  44.7 5.8 %copy-start.3 = (s32[1,1,128]{2,1,0:T(1,128)S(1)}, s32[1,1,128]{2,1,0:T(1,128)}, u32[]{:S(2)}) copy-start(s32[1,1,128]{2,1,0:T(1,128)} %param.15) | copy-start | bytes 1540
  45.4 25.1 %copy-start.1 = (bf16[128,256]{1,0:T(8,128)(2,1)S(1)}, bf16[128,256]{1,0:T(8,128)(2,1)}, u32[]{:S(2)}) copy-start(bf16[128,256]{1,0:T(8,128)(2,1)} %weight.1) | copy-start | bytes 196612
  45.4 25.1 %copy-start.2 = (bf16[128,256]{1,0:T(8,128)(2,1)S(1)}, bf16[128,256]{1,0:T(8,128)(2,1)}, u32[]{:S(2)}) copy-start(bf16[128,256]{1,0:T(8,128)(2,1)} %grad_out.1) | copy-start | bytes 196612
  45.4 25.1 %copy-start.4 = (f32[256]{0:T(256)S(1)}, f32[256]{0:T(256)}, u32[]{:S(2)}) copy-start(f32[256]{0:T(256)} %param.12) | copy-start | bytes 3076
  45.4 25.1 %copy-start.5 = (f32[128]{0:T(128)S(1)}, f32[128]{0:T(128)}, u32[]{:S(2)}) copy-start(f32[128]{0:T(128)} %param.11) | copy-start | bytes 1540
  52.2 3.4 %collective-permute-start.1 = (bf16[8,128,128]{2,1,0:T(8,128)(2,1)S(1)}, bf16[8,128,128]{2,1,0:T(8,128)(2,1)S(1)}, u32[]{:S(2)}, u32[]{:S(2)}) collective-permute-start(bf16[8,128,128]{2,1,0:T(8,128)(2,1)S(1)} %get-tuple-element.12), channel_id=1, source_target_pairs={{0,1},{1,0},{2,3},{3,2},{4,5},{5,4},{6,7},{7,6},{8,9},{9,8},{10,11... | collective-permute-start | bytes 786440 | tf_op jit(solution)/shard_map/ppermute | solution.py:205

commit v6 on v5

--- a/solution.py
+++ b/solution.py
@@ -27,7 +27,8 @@
 GW = 32
 PACK = E + GW
 CLASS = 8
-LINE = CLASS * E + GW
+GH = GW // 2
+LINE = CLASS * E + GH
 UNROLL = 64
 NCHIP = 8
 
@@ -132,11 +133,11 @@
     grad = packed[0, pl.ds(E, GW)].astype(F32)
     for k in range(1, NC):
         grad = grad + packed[k, pl.ds(E, GW)].astype(F32)
-    sent = grad.astype(BF16)
+    halves = [jnp.concatenate([grad[8 * x : 8 * x + 8], grad[16 + 8 * x : 24 + 8 * x]], axis=0) for x in range(NX)]
     for b in range(4):
         for k in range(CLASS):
             parts[b, pl.ds(k * E, E)] = total[b * CLASS + k].astype(BF16)
-        parts[b, pl.ds(CLASS * E, GW)] = sent
+        parts[b, pl.ds(CLASS * E, GH)] = halves[b // 2].astype(BF16)
 
 
 def class_kernel(parts, pack):
@@ -144,10 +145,10 @@
         first = parts[0, rows].astype(F32) + parts[1, rows].astype(F32)
         return (first + (parts[2, rows].astype(F32) + parts[3, rows].astype(F32))).astype(BF16)
 
-    share = value(pl.ds(CLASS * E, GW))
+    share = value(pl.ds(CLASS * E, GH))
     for k in range(CLASS):
         pack[k, pl.ds(0, E)] = value(pl.ds(k * E, E))
-        pack[k, pl.ds(E, GW)] = share
+        pack[k, pl.ds(E, GH)] = share
 
 
 def last_kernel(terms, grad_features, pieces):
@@ -155,8 +156,8 @@
     for k in range(1, CLASS):
         value = value + terms[k].astype(F32)
     grad_features[...] = value[:E].T.astype(BF16)
-    share = jnp.concatenate([value[E : E + 16], value[E + 16 :]], axis=1)
-    for k in range(NCHIP):
+    share = jnp.concatenate([value[E : E + 8], value[E + 8 :]], axis=1)
+    for k in range(NCHIP * NX):
         pieces[k] = share
 
 
@@ -235,7 +236,7 @@
     parts = lax.all_to_all(parts, QUAD, 0, 0, tiled=True)
     classes = pl.pallas_call(
         class_kernel,
-        out_shape=shape((CLASS, PACK, E)),
+        out_shape=shape((CLASS, E + GH, E)),
         in_specs=[VMEM],
         out_specs=VMEM,
         compiler_params=PARAMS,
@@ -244,13 +245,13 @@
     column = lax.all_to_all(classes, FAR, 0, 0, tiled=True)
     grad_features, pieces = pl.pallas_call(
         last_kernel,
-        out_shape=(shape((E, E)), shape((NCHIP, 16, WIDE), F32)),
+        out_shape=(shape((E, E)), shape((NCHIP * NX, 8, WIDE), F32)),
         in_specs=[VMEM],
         out_specs=(VMEM, VMEM),
         compiler_params=PARAMS,
         name="last_sum",
     )(column)
-    grad_weight = lax.all_to_all(pieces, CHIP, 0, 0, tiled=True).reshape(E, WIDE)
+    grad_weight = lax.all_to_all(pieces, CHIP + ("xl",), 0, 0, tiled=True).reshape(E, WIDE)
     return output, grad_features, grad_weight
 
 

time: 148 us -> 148 us (level)
  the two profiles are of different devices: /device:TPU:2 before, /device:TPU:32 now
where the time goes in v6:
time: 148 us; the launch traced here: 147 us
  blocking collectives  126 us (85%)
  waiting for transfers between devices  5.61 us (4%)
  Pallas kernels  5.48 us (4%)
  starting transfers between devices  5.31 us (4%)
  local copies, waits for them, and re-layouts  3.14 us (2%)
    all_gather x1, blocking collectives, on_device(): near = lax.all_gather(features, Z, axis=0, tiled=True).reshape(NZ, E, E)  36.3 us
    all_to_all x1, blocking collectives, on_device(): column = lax.all_to_all(classes, FAR, 0, 0, tiled=True)  28.2 us
    all_to_all x1, blocking collectives, on_device(): parts = lax.all_to_all(parts, QUAD, 0, 0, tiled=True)  19.7 us
    all_to_all x1, blocking collectives, on_device(): terms = lax.all_to_all(partial, CHIP, 0, 0, tiled=True)  15.7 us
    all_to_all x1, blocking collectives, on_device(): lax.all_to_all(pieces, CHIP + ('xl',), 0, 0, tiled=True).reshape(E, WIDE)  12 us
    all_to_all x1, blocking collectives, on_device(): packed = lax.all_to_all(pack, CHIP, 0, 0, tiled=True)  11.8 us
    ppermute x1, waiting for transfers between devices, on_device(): peer = lax.ppermute(near, 'xl', swap)  4.11 us
    ppermute x1, starting transfers between devices, on_device(): peer = lax.ppermute(near, 'xl', swap)  3.39 us
  transfers between devices with their start and end apart: 2, of which 2 were waited for; matrix products, arithmetic and copies ran while one was open for 0% of the time, Pallas kernels for 0%

profile of v6, /device:TPU:32, one launch (start us, length us, event | category | flops | bytes accessed | tf_op | source)
XLA Modules:
  0.0 147.0 jit_solution(8579472923686712377)
XLA Ops:
  0.6 36.3 %all_gather.6 = bf16[2048,128]{1,0:T(8,128)(2,1)S(1)} all-gather(bf16[128,128]{1,0:T(8,128)(2,1)} %param.9), channel_id=1, replica_groups=mesh['xl'=2,'zh'=4,'z1'=2,'z0'=2,'xh'=2,'y'=4,'core'=2] {'zh','z1','z0'}, dimensions={0}, use_global_device_ids=true | all-gather | bytes 557056 | tf_op jit(solution)/shard_map/all_gather | solution.py:179
  36.9 3.4 %collective-permute-start = (bf16[16,128,128]{2,1,0:T(8,128)(2,1)S(1)}, bf16[16,128,128]{2,1,0:T(8,128)(2,1)S(1)}, u32[]{:S(2)}, u32[]{:S(2)}) collective-permute-start(bf16[16,128,128]{2,1,0:T(8,128)(2,1)S(1)} %bitcast.38), channel_id=1, source_target_pairs={{0,256},{256,0},{1,257},{257,1},{2,258},{258,2},{3,259},{259,3},{4... | collective-permute-start | bytes 1572872 | tf_op jit(solution)/shard_map/ppermute | solution.py:180
  41.0 0.0 copy-start
  41.0 2.2 %copy-done = bf16[1,1,128,128,128]{4,3,2,1,0:T(8,128)(2,1)S(1)} copy-done((bf16[1,1,128,128,128]{4,3,2,1,0:T(8,128)(2,1)S(1)}, bf16[1,1,128,128,128]{4,3,2,1,0:T(8,128)(2,1)}, u32[]{:S(2)}) %copy-start) | copy-done | bytes 4194328
  43.2 0.0 copy-start.6
  43.2 0.0 copy-start.3
  43.2 0.4 preload.1.tiles
  43.5 0.3 copy-done.6
  43.8 0.0 copy-start.1
  43.8 0.0 copy-start.2
  43.8 0.0 copy-start.4
  43.8 0.0 copy-start.5
  43.9 4.1 %collective-permute-done.peer = bf16[16,128,128]{2,1,0:T(8,128)(2,1)S(1)} collective-permute-done((bf16[16,128,128]{2,1,0:T(8,128)(2,1)S(1)}, bf16[16,128,128]{2,1,0:T(8,128)(2,1)S(1)}, u32[]{:S(2)}, u32[]{:S(2)}) %collective-permute-start) | collective-permute-done | bytes 524320 | tf_op jit(solution)/shard_map/ppermute | solution.py:180
  48.0 0.0 copy-done.3
  48.0 1.7 %forward_sweep.1 = (bf16[8,128,128]{2,1,0:T(8,128)(2,1)S(1)}, bf16[8,128,128]{2,1,0:T(8,128)(2,1)S(1)}) custom-call(s32[1]{0:T(128)} %bitcast.35.count, s32[128]{0:T(128)S(1)} %bitcast.40, s32[128]{0:T(128)S(1)} %fusion.places, s32[1]{0:T(128)} %bitcast.3.core, bf16[128,128,128]{2,1,0:T(8,128)(2,1)S(1)} %preload.1.tiles, bf16[16,128,128]{2,1,0:T(8,128)(2,1)S(1)} %bitcast.39, ...), custom_call_target="tpu_custom_call" | custom-call | tf_op jit(solution)/shard_map/forward_sweep/pallas_call | solution.py:193
  49.6 1.9 %collective-permute-start.1 = (bf16[8,128,128]{2,1,0:T(8,128)(2,1)S(1)}, bf16[8,128,128]{2,1,0:T(8,128)(2,1)S(1)}, u32[]{:S(2)}, u32[]{:S(2)}) collective-permute-start(bf16[8,128,128]{2,1,0:T(8,128)(2,1)S(1)} %get-tuple-element.12), channel_id=1, source_target_pairs={{0,1},{1,0},{2,3},{3,2},{4,5},{5,4},{6,7},{7,6},{8,9},{9,8},{10,11... | collective-permute-start | bytes 786440 | tf_op jit(solution)/shard_map/ppermute | solution.py:206
  51.6 1.5 %collective-permute-done.1.far = bf16[8,128,128]{2,1,0:T(8,128)(2,1)S(1)} collective-permute-done((bf16[8,128,128]{2,1,0:T(8,128)(2,1)S(1)}, bf16[8,128,128]{2,1,0:T(8,128)(2,1)S(1)}, u32[]{:S(2)}, u32[]{:S(2)}) %collective-permute-start.1) | collective-permute-done | bytes 262176 | tf_op jit(solution)/shard_map/ppermute | solution.py:206
  53.1 0.1 chip_sum.1
  53.1 15.7 %all_to_all.25.terms = bf16[8,128,128]{2,1,0:T(8,128)(2,1)S(1)} all-to-all(bf16[8,128,128]{2,1,0:T(8,128)(2,1)S(1)} %chip_sum.1), channel_id=1, replica_groups=mesh['xl'=2,'zh'=4,'z1'=2,'z0'=2,'xh'=2,'y'=4,'core'=2] {'xh','y'}, dimensions={0} | all-to-all | bytes 524288 | tf_op jit(solution)/shard_map/all_to_all | solution.py:215
  68.9 0.0 copy-done.1
  68.9 0.0 copy-done.2
  68.9 0.0 copy-done.4
  68.9 0.0 copy-done.5
  68.9 0.9 node_update.1
  69.8 11.8 %all_to_all.26 = bf16[8,160,128]{2,1,0:T(8,128)(2,1)S(1)} all-to-all(bf16[8,160,128]{2,1,0:T(8,128)(2,1)S(1)} %get-tuple-element.14), channel_id=1, replica_groups=mesh['xl'=2,'zh'=4,'z1'=2,'z0'=2,'xh'=2,'y'=4,'core'=2] {'xh','y'}, dimensions={0} | all-to-all | bytes 655360 | tf_op jit(solution)/shard_map/all_to_all | solution.py:224
  81.6 2.3 %all_gather.7.packed = bf16[16,160,128]{2,1,0:T(8,128)(2,1)S(1)} all-gather(bf16[8,160,128]{2,1,0:T(8,128)(2,1)S(1)} %all_to_all.26), channel_id=1, replica_groups=mesh['xl'=2,'zh'=4,'z1'=2,'z0'=2,'xh'=2,'y'=4,'core'=2] {'core'}, dimensions={0}, use_global_device_ids=true | all-gather | bytes 983040 | tf_op jit(solution)/shard_map/all_gather | solution.py:225
  83.9 1.7 %backward_sweep.1 = bf16[4,1040,128]{2,1,0:T(8,128)(2,1)S(1)} custom-call(s32[1]{0:T(128)} %bitcast.36.count, s32[128]{0:T(128)S(1)} %bitcast.41, s32[128]{0:T(128)S(1)} %get-tuple-element.17.places, bf16[128,128,128]{2,1,0:T(8,128)(2,1)S(1)} %preload.1.tiles, bf16[16,160,128]{2,1,0:T(8,128)(2,1)S(1)} %all_gather.7.packed), custom_call_target="tpu_custom_call" | custom-call | tf_op jit(solution)/shard_map/backward_sweep/pallas_call | solution.py:227
  85.6 19.7 %all_to_all.27.parts = bf16[4,1040,128]{2,1,0:T(8,128)(2,1)S(1)} all-to-all(bf16[4,1040,128]{2,1,0:T(8,128)(2,1)S(1)} %backward_sweep.1), channel_id=1, replica_groups=mesh['xl'=2,'zh'=4,'z1'=2,'z0'=2,'xh'=2,'y'=4,'core'=2] {'xl','z0'}, dimensions={0} | all-to-all | bytes 2129920 | tf_op jit(solution)/shard_map/all_to_all | solution.py:236
  105.2 0.1 class_sum.1
  105.3 28.2 %all_to_all.28.terms = bf16[8,144,128]{2,1,0:T(8,128)(2,1)S(1)} all-to-all(bf16[8,144,128]{2,1,0:T(8,128)(2,1)S(1)} %class_sum.1), channel_id=1, replica_groups=mesh['xl'=2,'zh'=4,'z1'=2,'z0'=2,'xh'=2,'y'=4,'core'=2] {'zh','z1'}, dimensions={0} | all-to-all | bytes 589824 | tf_op jit(solution)/shard_map/all_to_all | solution.py:245
  133.5 0.7 last_sum.1
  134.3 12.0 %all_to_all.29 = f32[16,8,256]{2,1,0:T(8,128)S(1)} all-to-all(f32[16,8,256]{2,1,0:T(8,128)S(1)} %get-tuple-element.16), channel_id=1, replica_groups=mesh['xl'=2,'zh'=4,'z1'=2,'z0'=2,'xh'=2,'y'=4,'core'=2] {'xh','y','xl'}, dimensions={0} | all-to-all | bytes 262144 | tf_op jit(solution)/shard_map/all_to_all | solution.py:254
  146.3 0.7 copy.14
  (2 shorter events, 0.0 us)
Async XLA Ops:
  36.9 11.1 %collective-permute-start = (bf16[16,128,128]{2,1,0:T(8,128)(2,1)S(1)}, bf16[16,128,128]{2,1,0:T(8,128)(2,1)S(1)}, u32[]{:S(2)}, u32[]{:S(2)}) collective-permute-start(bf16[16,128,128]{2,1,0:T(8,128)(2,1)S(1)} %bitcast.38), channel_id=1, source_target_pairs={{0,256},{256,0},{1,257},{257,1},{2,258},{258,2},{3,259},{259,3},{4... | collective-permute-start | bytes 1572872 | tf_op jit(solution)/shard_map/ppermute | solution.py:180
  41.0 2.2 %copy-start = (bf16[1,1,128,128,128]{4,3,2,1,0:T(8,128)(2,1)S(1)}, bf16[1,1,128,128,128]{4,3,2,1,0:T(8,128)(2,1)}, u32[]{:S(2)}) copy-start(bf16[1,1,128,128,128]{4,3,2,1,0:T(8,128)(2,1)} %param.14) | copy-start | bytes 12582916
  43.2 0.7 copy-start.6
  43.2 4.8 %copy-start.3 = (s32[1,1,128]{2,1,0:T(1,128)S(1)}, s32[1,1,128]{2,1,0:T(1,128)}, u32[]{:S(2)}) copy-start(s32[1,1,128]{2,1,0:T(1,128)} %param.15) | copy-start | bytes 1540
  43.8 25.1 %copy-start.1 = (bf16[128,256]{1,0:T(8,128)(2,1)S(1)}, bf16[128,256]{1,0:T(8,128)(2,1)}, u32[]{:S(2)}) copy-start(bf16[128,256]{1,0:T(8,128)(2,1)} %weight.1) | copy-start | bytes 196612
  43.8 25.1 %copy-start.2 = (bf16[128,256]{1,0:T(8,128)(2,1)S(1)}, bf16[128,256]{1,0:T(8,128)(2,1)}, u32[]{:S(2)}) copy-start(bf16[128,256]{1,0:T(8,128)(2,1)} %grad_out.1) | copy-start | bytes 196612
  43.8 25.1 %copy-start.4 = (f32[256]{0:T(256)S(1)}, f32[256]{0:T(256)}, u32[]{:S(2)}) copy-start(f32[256]{0:T(256)} %param.12) | copy-start | bytes 3076
  43.8 25.1 %copy-start.5 = (f32[128]{0:T(128)S(1)}, f32[128]{0:T(128)}, u32[]{:S(2)}) copy-start(f32[128]{0:T(128)} %param.11) | copy-start | bytes 1540
  49.6 3.4 %collective-permute-start.1 = (bf16[8,128,128]{2,1,0:T(8,128)(2,1)S(1)}, bf16[8,128,128]{2,1,0:T(8,128)(2,1)S(1)}, u32[]{:S(2)}, u32[]{:S(2)}) collective-permute-start(bf16[8,128,128]{2,1,0:T(8,128)(2,1)S(1)} %get-tuple-element.12), channel_id=1, source_target_pairs={{0,1},{1,0},{2,3},{3,2},{4,5},{5,4},{6,7},{7,6},{8,9},{9,8},{10,11... | collective-permute-start | bytes 786440 | tf_op jit(solution)/shard_map/ppermute | solution.py:206
